TPU v7x, 32 devices: a whole 2x2x4 slice. The times are simulated.
32 devices in a mesh: graph: 4 (over z), feat: 8 (over y, x, core).
Axes of the slice: x: 2, y: 2, z: 4, core: 2. Of those that a mesh axis runs over, the one named last changes fastest.
Arguments:
- node_features: bfloat16 [32768, 1024], P('graph', 'feat'), may hold values from -6 to 6
- proj_weight: bfloat16 [1024, 512], P('feat'), may hold values from -0.1875 to 0.1875
- relation_weight: bfloat16 [2, 512, 512], replicated, may hold values from -0.25 to 0.25
- att_source: float32 [2, 512], replicated, may hold values from -8 to 8
- att_target: float32 [2, 512], replicated, may hold values from -8 to 8
- edge_mask: int32 [256, 12, 128, 128], P(('graph', 'feat')), may hold values from 0 to 1, as said below
- relation_ids: int32 [256, 12], P(('graph', 'feat')), may hold values from 0 to 1
- send_blocks: int32 [32, 4, 4], P(('graph', 'feat')), may hold values from 0 to 7, as said below
- source_slots: int32 [256, 12], P(('graph', 'feat')), may hold values from 0 to 15
Outputs:
- layer_out: bfloat16 [32768, 512], P(('graph', 'feat'))
Inputs may be any that keep to these rules, and one draw needn't show every extreme that they name: `edge_mask`: every target row i has an edge at list position 0 to row i of that source block. `send_blocks`: the 4 entries of one device's list to one graph index are distinct block numbers of that device.
All inputs are finite; a program needn't handle non-finite values.
Results may differ from a plain program's by a relative error of at most 0.034.
Values may be sent and summed in bfloat16 or wider, within the bound.
A program may use at most 128 MiB of HBM per device.

v0:
```python
import jax
import jax.numpy as jnp
from jax import lax
from jax.sharding import PartitionSpec as P

HEADS = 4


def attend(target_scores, source_scores, live, values, own):
    heads_count = target_scores.shape[1]
    width = values.shape[2]
    lists = target_scores.shape[0]
    rows = target_scores.shape[2]
    lhs = jnp.transpose(target_scores, (1, 2, 0))
    rhs = jnp.transpose(source_scores, (1, 0, 2))
    raw = lhs[:, :, :, None] + rhs[:, None, :, :]
    leaky = jnp.where(raw > 0, raw, 0.2 * raw)
    usable = (jnp.transpose(live, (1, 0, 2)) > 0)[None]
    masked = jnp.where(usable, leaky, -jnp.inf)
    highest = jnp.max(masked, axis=(2, 3), keepdims=True)
    prob = jnp.exp(masked - highest)
    total = jnp.sum(prob, axis=(2, 3))
    weights = prob.astype(jnp.bfloat16).reshape(heads_count, rows, lists * values.shape[1])
    stacked = values.reshape(lists * values.shape[1], heads_count, width // heads_count)
    summed = jnp.einsum("hix,xhd->hid", weights, stacked, preferred_element_type=jnp.float32)
    summed = summed / total[:, :, None]
    mixed = jnp.transpose(summed, (1, 0, 2)).reshape(rows, width) + own.astype(jnp.float32)
    return jax.nn.elu(mixed).astype(jnp.bfloat16)


def shards(
    node_features,
    proj_weight,
    relation_weight,
    att_source,
    att_target,
    edge_mask,
    relation_ids,
    send_blocks,
    source_slots,
):
    block_rows = edge_mask.shape[-1]
    local_blocks = edge_mask.shape[0]
    rows_local = local_blocks * block_rows
    width = proj_weight.shape[1]
    head_width = width // HEADS
    relations = relation_weight.shape[0]
    hidden = lax.psum_scatter(
        jnp.dot(node_features, proj_weight, preferred_element_type=jnp.float32),
        "feat",
        scatter_dimension=0,
        tiled=True,
    ).astype(jnp.bfloat16)
    blocks = hidden.reshape(local_blocks, block_rows, width)
    outgoing = blocks[send_blocks[0]]
    src_att = att_source.reshape(relations, 1, HEADS, head_width)
    transform_values = jnp.einsum(
        "gnrc,scd->gnsrd",
        lax.all_to_all(outgoing, "graph", split_axis=0, concat_axis=0, tiled=True),
        relation_weight,
        preferred_element_type=jnp.float32,
    ).astype(jnp.bfloat16)
    split_heads = transform_values.astype(jnp.float32).reshape(
        transform_values.shape[:4] + (HEADS, head_width)
    )
    scores = jnp.sum(split_heads * src_att[None, None], axis=-1)
    values = transform_values
    source_all = jnp.transpose(scores, (0, 1, 2, 4, 3))
    slots_total = values.shape[0] * values.shape[1]
    values = values.reshape((slots_total,) + values.shape[2:])
    source_all = source_all.reshape((slots_total,) + source_all.shape[2:])
    own_heads = blocks.astype(jnp.float32).reshape(local_blocks, block_rows, HEADS, head_width)
    tgt_att = att_target.reshape(relations, HEADS, head_width)
    target_all = jnp.sum(own_heads[:, None] * tgt_att[None, :, None], axis=-1)

    def one_block(inputs):
        target_block, live, rels, slots, own = inputs
        chosen = values[slots, rels]
        source_scores = source_all[slots, rels]
        target_scores = jnp.transpose(target_block[rels], (0, 2, 1))
        return attend(target_scores, source_scores, live, chosen, own)

    result = lax.map(one_block, (target_all, edge_mask, relation_ids, source_slots, blocks))
    return result.reshape(rows_local, width)


def solution(mesh):
    placed = (
        P("graph", "feat"),
        P("feat", None),
        P(),
        P(),
        P(),
        P(("graph", "feat"), None, None, None),
        P(("graph", "feat"), None),
        P(("graph", "feat"), None, None),
        P(("graph", "feat"), None),
    )
    return jax.shard_map(
        shards, mesh=mesh, in_specs=placed, out_specs=P(("graph", "feat"), None), check_vma=False
    )
```

profile of v0, /device:TPU:0, one launch (start us, length us, event | category | flops | bytes accessed | tf_op | source)
XLA Modules:
  0.0 345.6 jit_solution(12027837647494873527)
XLA Ops:
  6.5 1.6 copy-done
  8.1 8.9 %fusion.21 = f32[8192,512]{1,0:T(8,128)} fusion(bf16[8192,128]{1,0:T(8,128)(2,1)S(1)} %copy-done, bf16[128,512]{1,0:T(8,128)(2,1)} %param.12), kind=kOutput, calls=%fused_computation.45 | convolution fusion | flops 1073741824 | bytes 19005440 | tf_op jit(solution)/shard_map/dot_general | solution.py:49
  17.9 118.1 %reduce-scatter.2.cloned.1.call-done = f32[1024,512]{1,0:T(8,128)} async-done(((f32[8192,512]{1,0:T(8,128)}), f32[1024,512]{1,0:T(8,128)}) %reduce-scatter.2.cloned.1.call-update) | async-done | bytes 2097168 | tf_op jit(solution)/shard_map/reduce_scatter | solution.py:48
  135.9 1.7 convert_element_type.32
  137.6 2.0 gather_fusion.3
  139.7 4.7 %all-to-all-start = ((bf16[4,4,128,512]{3,2,1,0:T(8,128)(2,1)}), bf16[4,4,128,512]{3,2,1,0:T(8,128)(2,1)S(1)}, u32[]{:S(2)}, u32[]{:S(2)}) async-start(bf16[4,4,128,512]{3,2,1,0:T(8,128)(2,1)} %bitcast.108), calls=%async_computation.1 | async-start | bytes 4194304 | tf_op jit(solution)/shard_map/all_to_all | solution.py:59
  144.4 1.7 reshape.137
  146.1 1.9 copy.34
  148.0 1.2 multiply_reduce_fusion.1
  149.2 43.4 %all-to-all-done = bf16[4,4,128,512]{3,2,1,0:T(8,128)(2,1)S(1)} async-done(((bf16[4,4,128,512]{3,2,1,0:T(8,128)(2,1)}), bf16[4,4,128,512]{3,2,1,0:T(8,128)(2,1)S(1)}, u32[]{:S(2)}, u32[]{:S(2)}) %all-to-all-start) | async-done | bytes 2097184 | tf_op jit(solution)/shard_map/all_to_all | solution.py:59
  192.6 8.0 %bitcast_convert_fusion = (f32[4,4,2,128,512]{4,3,2,1,0:T(8,128)}, bf16[4,4,128,2,512]{4,2,3,1,0:T(8,128)(2,1)}) fusion(bf16[2,512,512]{2,1,0:T(8,128)(2,1)} %param.13, bf16[4,4,128,512]{3,2,1,0:T(8,128)(2,1)S(1)} %all-to-all-done), kind=kOutput, calls=%fused_computation.38 | convolution fusion | flops 2151677952 | bytes 15728640 | tf_op jit(solution)/shard_map/gnrc,scd->gnsrd/dot_general | solution.py:57
  200.6 9.9 %reshape.139 = f32[4,4,2,128,4,128]{5,4,3,2,1,0:T(4,128)} reshape(f32[4,4,2,128,512]{4,3,2,1,0:T(8,128)} %get-tuple-element.109) | data formatting | bytes 16777216 | tf_op jit(solution)/shard_map/reshape | solution.py:63
  210.5 7.9 %multiply_reduce_fusion = f32[4,4,2,128,4]{4,3,2,1,0:T(8,128)S(1)} fusion(f32[4,4,2,128,4,128]{5,4,3,2,1,0:T(4,128)} %reshape.139, f32[2,4,128]{2,1,0:T(4,128)S(1)} %mul.35), kind=kLoop, calls=%fused_computation.37 | loop fusion | flops 4177920 | bytes 8458240 | tf_op jit(solution)/shard_map/reduce_sum | solution.py:66
  219.0 118.2 %while.10 = (s32[]{:T(128)}, bf16[8,128,512]{2,1,0:T(8,128)(2,1)}, s32[8,12,128,128]{3,2,1,0:T(8,128)}, f32[8,2,128,4]{2,3,1,0:T(4,128)S(1)}, s32[8,12]{1,0:T(8,...) while((s32[]{:T(128)}, bf16[8,128,512]{2,1,0:T(8,128)(2,1)}, ...), condition=%wide.region_6.7_spmd, body=%wide.region_3.6_spmd.sunk | while | flops 217907328 | bytes 27303052 | solution.py:83
  219.0 0.8 fusion.36
  221.3 1.2 constant_dynamic-slice_fusion.6
  222.8 1.0 fusion.38
  223.8 1.2 exponential_reduce_fusion.2
  225.2 2.1 fusion.39
  227.3 2.8 gather_fusion.2
  230.6 2.1 fusion.40
  236.0 1.2 constant_dynamic-slice_fusion.6
  237.6 1.0 fusion.38
  238.6 1.2 exponential_reduce_fusion.2
  240.0 2.1 fusion.39
  242.1 2.8 gather_fusion.2
  245.4 2.1 fusion.40
  250.8 1.2 constant_dynamic-slice_fusion.6
  252.4 1.0 fusion.38
  253.4 1.2 exponential_reduce_fusion.2
  254.8 2.1 fusion.39
  256.9 2.8 gather_fusion.2
  260.1 2.1 fusion.40
  265.6 1.2 constant_dynamic-slice_fusion.6
  267.2 1.0 fusion.38
  268.2 1.2 exponential_reduce_fusion.2
  269.5 2.1 fusion.39
  271.6 2.8 gather_fusion.2
  274.9 2.1 fusion.40
  280.3 1.2 constant_dynamic-slice_fusion.6
  281.9 1.0 fusion.38
  282.9 1.2 exponential_reduce_fusion.2
  284.3 2.1 fusion.39
  286.4 2.8 gather_fusion.2
  289.7 2.1 fusion.40
  295.1 1.2 constant_dynamic-slice_fusion.6
  296.7 1.0 fusion.38
  297.7 1.2 exponential_reduce_fusion.2
  299.1 2.1 fusion.39
  301.2 2.8 gather_fusion.2
  304.5 2.1 fusion.40
  309.9 1.2 constant_dynamic-slice_fusion.6
  311.5 1.0 fusion.38
  312.5 1.2 exponential_reduce_fusion.2
  313.8 2.1 fusion.39
  315.9 2.8 gather_fusion.2
  319.2 2.1 fusion.40
  324.7 1.2 constant_dynamic-slice_fusion.6
  326.2 1.0 fusion.38
  327.2 1.2 exponential_reduce_fusion.2
  328.6 2.1 fusion.39
  330.7 2.8 gather_fusion.2
  334.0 2.1 fusion.40
  337.2 1.6 copy-done.1
  (176 shorter events, 34.0 us)
Async XLA Ops:
  6.5 1.6 copy-start
  6.5 129.4 %reduce-scatter.2.cloned.1.call-start = ((), (), s32[]{:S(2)}) async-start(), calls=%async_computation.2 | async-start | bytes 18874368 | tf_op jit(solution)/shard_map/reduce_scatter | solution.py:48
  17.1 0.7 copy-start.6
  139.7 4.7 %copy-start.4 = (f32[2,512]{1,0:T(2,128)S(1)}, f32[2,512]{1,0:T(2,128)}, u32[]{:S(2)}) copy-start(f32[2,512]{1,0:T(2,128)} %param.14) | copy-start | bytes 12292
  139.7 4.8 %copy-start.5 = (f32[2,512]{1,0:T(2,128)S(1)}, f32[2,512]{1,0:T(2,128)}, u32[]{:S(2)}) copy-start(f32[2,512]{1,0:T(2,128)} %param.15) | copy-start | bytes 12292
  139.7 52.9 %all-to-all-start = ((bf16[4,4,128,512]{3,2,1,0:T(8,128)(2,1)}), bf16[4,4,128,512]{3,2,1,0:T(8,128)(2,1)S(1)}, u32[]{:S(2)}, u32[]{:S(2)}) async-start(bf16[4,4,128,512]{3,2,1,0:T(8,128)(2,1)} %bitcast.108), calls=%async_computation.1 | async-start | bytes 4194304 | tf_op jit(solution)/shard_map/all_to_all | solution.py:59
  219.0 1.0 copy-start.2
  230.6 2.1 copy-start.3
  233.8 1.0 copy-start.2
  245.4 2.1 copy-start.3
  248.6 1.0 copy-start.2
  260.1 2.1 copy-start.3
  263.4 1.0 copy-start.2
  274.9 2.1 copy-start.3
  278.1 1.0 copy-start.2
  289.7 2.1 copy-start.3
  292.9 1.0 copy-start.2
  304.4 2.1 copy-start.3
  307.7 1.0 copy-start.2
  319.2 2.1 copy-start.3
  322.4 1.0 copy-start.2
  334.0 2.1 copy-start.3
  337.2 1.6 copy-start.1
Sparse Core Ops, SparseCore 0:
  17.2 118.6 reduce-scatter.1
where the time goes:
time: 348 us; the launch traced here: 346 us
  waiting for transfers between devices  161 us (46%)
  local copies, waits for them, and re-layouts  76.7 us (22%)
  other arithmetic  54.5 us (16%)
  matrix products  33.9 us (10%)
  between operations  13.4 us (4%)
  starting transfers between devices  4.74 us (1%)
    reduce_scatter x1, waiting for transfers between devices, shards(): lax.psum_scatter(jnp.dot(node_features, proj_weight, preferred_element_ty...  118 us
    all_to_all x1, waiting for transfers between devices, shards(): lax.all_to_all(outgoing, 'graph', split_axis=0, concat_axis=0, tiled=True)  43.4 us
    gather x8, local copies, waits for them, and re-layouts, one_block(): chosen = values[slots, rels]  22.7 us
    dot_general x8, matrix products, attend(): jnp.einsum('hix,xhd->hid', weights, stacked, preferred_element_type=jnp.f...  16.9 us
    convert_element_type x8, other arithmetic, attend(): prob.astype(jnp.bfloat16)  16.8 us
    dynamic_slice x32, local copies, waits for them, and re-layouts, shards(): lax.map(one_block, (target_all, edge_mask, relation_ids, source_slots, bl...  12.7 us
    reduce_sum x8, other arithmetic, attend(): total = jnp.sum(prob, axis=(2, 3))  9.97 us
    reshape x1, local copies, waits for them, and re-layouts, shards(): transform_values.astype(jnp.float32)  9.92 us
  transfers between devices with their start and end apart: 2, of which 2 were waited for; matrix products, arithmetic and copies ran while one was open for 1% of the time, Pallas kernels for 0%

commit v1 on v0

v1 whole, which is shorter than its diff:
```python
import functools
import math

import jax
import jax.numpy as jnp
from jax import lax
from jax.experimental import pallas as pl
from jax.experimental.pallas import tpu as pltpu
from jax.sharding import PartitionSpec as P

HEADS = 4
LOG2E = math.log2(math.e)
NT = (((1,), (1,)), ((), ()))


def split_bf16(x):
    hi = x.astype(jnp.bfloat16)
    lo = (x - hi.astype(jnp.float32)).astype(jnp.bfloat16)
    return hi, lo


def hidden_kernel(x_ref, w_ref, out_ref):
    total = jnp.dot(x_ref[0], w_ref[0], preferred_element_type=jnp.float32)
    for f in range(1, x_ref.shape[0]):
        total += jnp.dot(x_ref[f], w_ref[f], preferred_element_type=jnp.float32)
    out_ref[...] = total.astype(out_ref.dtype)


def project(x, w):
    feats, rows, depth = x.shape
    width = w.shape[2]
    tile = min(rows, 256)
    return pl.pallas_call(
        hidden_kernel,
        grid=(rows // tile,),
        in_specs=[
            pl.BlockSpec((feats, tile, depth), lambda i: (0, i, 0)),
            pl.BlockSpec((feats, depth, width), lambda i: (0, 0, 0)),
        ],
        out_specs=pl.BlockSpec((tile, width), lambda i: (i, 0)),
        out_shape=jax.ShapeDtypeStruct((rows, width), jnp.bfloat16),
        compiler_params=pltpu.CompilerParams(vmem_limit_bytes=40 << 20),
        name="project",
    )(x, w)


def attention_kernel(
    rels_ref,
    slots_ref,
    front_ref,
    own_ref,
    relw_ref,
    atts_ref,
    attt_ref,
    mask_ref,
    out_ref,
    values,
    scores,
    tatt,
    target,
    stack,
    raws,
    bias,
    weights,
):
    slots = front_ref.shape[0]
    rows = front_ref.shape[1]
    width = front_ref.shape[2]
    hw = width // HEADS
    relations = relw_ref.shape[0]
    lists = mask_ref.shape[1]
    b = pl.program_id(0)

    @pl.when(b == 0)
    def _():
        head_of = lax.broadcasted_iota(jnp.int32, (8, width), 1) // hw
        row_of = lax.broadcasted_iota(jnp.int32, (8, width), 0)
        for r in range(relations):
            hi, lo = split_bf16(atts_ref[r : r + 1, :] * LOG2E)
            parts = [
                jnp.where(head_of == row_of, part.astype(jnp.float32), 0.0)
                for part in (hi, lo)
            ]
            att = jnp.concatenate(parts, axis=0).astype(jnp.bfloat16)

            def one_slot(s, carry):
                v = jnp.dot(
                    front_ref[s], relw_ref[r], preferred_element_type=jnp.float32
                ).astype(jnp.bfloat16)
                values[r * slots + s] = v
                both = lax.dot_general(att, v, NT, preferred_element_type=jnp.float32)
                scores[r * slots + s] = both[:8] + both[8:]
                return carry

            lax.fori_loop(0, slots, one_slot, 0)
            hi, lo = split_bf16(attt_ref[r : r + 1, :] * LOG2E)
            for n, part in enumerate((hi, lo)):
                tatt[n, r * rows : (r + 1) * rows, :] = jnp.broadcast_to(
                    part.astype(jnp.float32), (rows, width)
                ).astype(jnp.bfloat16)
        stack[:, :, hw:] = jnp.ones((HEADS, lists * rows, hw), jnp.bfloat16)

    index = []
    for k in range(lists):
        rel = rels_ref[b, k]
        index.append((rel, rel * slots + slots_ref[b, k]))
    for k in range(lists):
        v = values[index[k][1]]
        for h in range(HEADS):
            stack[h, k * rows : (k + 1) * rows, :hw] = v[:, h * hw : (h + 1) * hw]
        bias[k] = jnp.where(mask_ref[0, k] > 0, 0.0, -jnp.inf)
    for h in range(HEADS):
        cols = slice(h * hw, (h + 1) * hw)
        own = own_ref[:, cols]
        both = lax.dot_general(
            own, tatt[0, :, cols], NT, preferred_element_type=jnp.float32
        ) + lax.dot_general(own, tatt[1, :, cols], NT, preferred_element_type=jnp.float32)
        for r in range(relations):
            target[r] = both[:, r * rows : (r + 1) * rows]
        top = None
        for k in range(lists):
            rel, place = index[k]
            raw = (target[rel] + scores[place, h : h + 1, :]) + bias[k]
            raws[k] = raw
            top = raw if top is None else jnp.maximum(top, raw)
        top = jnp.max(top, axis=1, keepdims=True)
        top = jnp.broadcast_to(jnp.maximum(top, 0.2 * top), (rows, rows))
        for k in range(lists):
            raw = raws[k]
            prob = jnp.exp2(jnp.maximum(raw, 0.2 * raw) - top)
            weights[:, k * rows : (k + 1) * rows] = prob.astype(jnp.bfloat16)
        summed = jnp.dot(weights[...], stack[h], preferred_element_type=jnp.float32)
        mixed = summed[:, :hw] / summed[:, hw:] + own.astype(jnp.float32)
        out_ref[:, cols] = jnp.where(
            mixed > 0, mixed, jnp.exp(jnp.minimum(mixed, 0.0)) - 1.0
        ).astype(out_ref.dtype)


def attention(rels, slots, front, hidden, relw, atts, attt, mask):
    count, rows, width = front.shape
    blocks, lists = mask.shape[:2]
    relations = relw.shape[0]
    hw = width // HEADS
    smem = pl.BlockSpec(memory_space=pltpu.SMEM)
    whole = pl.BlockSpec(memory_space=pltpu.VMEM)
    return pl.pallas_call(
        attention_kernel,
        grid=(blocks,),
        in_specs=[
            smem,
            smem,
            whole,
            pl.BlockSpec((rows, width), lambda b: (b, 0)),
            whole,
            whole,
            whole,
            pl.BlockSpec((1, lists, rows, rows), lambda b: (b, 0, 0, 0)),
        ],
        out_specs=pl.BlockSpec((rows, width), lambda b: (b, 0)),
        out_shape=jax.ShapeDtypeStruct((blocks * rows, width), jnp.bfloat16),
        scratch_shapes=[
            pltpu.VMEM((relations * count, rows, width), jnp.bfloat16),
            pltpu.VMEM((relations * count, 8, rows), jnp.float32),
            pltpu.VMEM((2, relations * rows, width), jnp.bfloat16),
            pltpu.VMEM((relations, rows, rows), jnp.float32),
            pltpu.VMEM((HEADS, lists * rows, 2 * hw), jnp.bfloat16),
            pltpu.VMEM((lists, rows, rows), jnp.float32),
            pltpu.VMEM((lists, rows, rows), jnp.float32),
            pltpu.VMEM((rows, lists * rows), jnp.bfloat16),
        ],
        compiler_params=pltpu.CompilerParams(vmem_limit_bytes=56 << 20),
        name="attention",
    )(rels, slots, front, hidden, relw, atts, attt, mask)


def shards(x, w, relw, atts, attt, mask, rels, send, slots):
    rows = mask.shape[-1]
    blocks = mask.shape[0]
    feats = x.shape[0] // (blocks * rows)
    x = x.reshape(feats, blocks * rows, x.shape[1])
    x = lax.all_to_all(x, "feat", split_axis=0, concat_axis=0, tiled=True)
    w = lax.all_gather(w, "feat", axis=0)
    hidden = project(x, w)
    out = hidden.reshape(blocks, rows, -1)[send[0]]
    front = lax.all_to_all(out, "graph", split_axis=0, concat_axis=0, tiled=True)
    front = front.reshape((-1,) + front.shape[2:])
    return attention(rels, slots, front, hidden, relw, atts, attt, mask)


def solution(mesh):
    placed = (
        P("graph", "feat"),
        P("feat", None),
        P(),
        P(),
        P(),
        P(("graph", "feat"), None, None, None),
        P(("graph", "feat"), None),
        P(("graph", "feat"), None, None),
        P(("graph", "feat"), None),
    )
    return jax.shard_map(
        shards, mesh=mesh, in_specs=placed, out_specs=P(("graph", "feat"), None), check_vma=False
    )
```

time: 348 us -> 142 us (0.41)
  waiting for transfers between devices: 161 us -> 33 us
  local copies, waits for them, and re-layouts: 76.7 us -> 2.28 us
  other arithmetic: 54.5 us -> 0.01 us
  blocking collectives: 0 us -> 53.4 us
  Pallas kernels: 0 us -> 34.3 us
  matrix products: 33.9 us -> 0 us
    reduce_scatter x1 -> x0, waiting for transfers between devices: 118 us -> none  [shards(): lax.psum_scatter(jnp.dot(node_features, proj_weight, preferred_element_ty...]
    all_to_all x0 -> x1, blocking collectives: none -> 53.4 us  [shards(): lax.all_to_all(out, 'graph', split_axis=0, concat_axis=0, tiled=True)]
    all_to_all x1, waiting for transfers between devices: 43.4 us -> 0.01 us  [shards(): x = lax.all_to_all(x, 'feat', split_axis=0, concat_axis=0, tiled=True)]
    pallas_call x0 -> x2, Pallas kernels: none -> 34.3 us  [the longest x1 31.4 us: attention(): pl.pallas_call(attention_kernel, grid=(blocks,), in_specs=[smem, smem, wh...]
    gather x25 -> x1, local copies, waits for them, and re-layouts: 34.6 us -> 0.68 us  [shards(): out = hidden.reshape(blocks, rows, -1)[send[0]]]
    dot_general x10 -> x0, matrix products: 33.9 us -> none  [the longest x8 16.9 us: attend(): jnp.einsum('hix,xhd->hid', weights, stacked, preferred_element_type=jnp.f...]
    all_gather x0 -> x1, waiting for transfers between devices: none -> 32.3 us  [shards(): w = lax.all_gather(w, 'feat', axis=0)]
    convert_element_type x17 -> x0, other arithmetic: 19.6 us -> none  [the longest x8 16.8 us: attend(): prob.astype(jnp.bfloat16)]
  transfers between devices with their start and end apart: 2 -> 2, of which waited for: 2 -> 1; matrix products, arithmetic and copies ran while one was open for 1% -> 0% of each run, Pallas kernels for 0% -> 0%
where the time goes in v1:
time: 142 us
  blocking collectives  53.4 us (38%)
  Pallas kernels  34.3 us (24%)
  waiting for transfers between devices  33 us (23%)
  between operations  13.4 us (9%)
  starting transfers between devices  5.18 us (4%)
  local copies, waits for them, and re-layouts  2.28 us (2%)
    all_to_all x1, blocking collectives, shards(): lax.all_to_all(out, 'graph', split_axis=0, concat_axis=0, tiled=True)  53.4 us
    all_gather x1, waiting for transfers between devices, shards(): w = lax.all_gather(w, 'feat', axis=0)  32.3 us
    pallas_call x1, Pallas kernels, attention(): pl.pallas_call(attention_kernel, grid=(blocks,), in_specs=[smem, smem, wh...  31.4 us
    all_to_all x1, starting transfers between devices, shards(): x = lax.all_to_all(x, 'feat', split_axis=0, concat_axis=0, tiled=True)  5.18 us
    pallas_call x1, Pallas kernels, project(): pl.pallas_call(hidden_kernel, grid=(rows // tile,), in_specs=[pl.BlockSpe...  2.92 us
  transfers between devices with their start and end apart: 2, of which 1 were waited for; matrix products, arithmetic and copies ran while one was open for 0% of the time, Pallas kernels for 0%

profile of v1, /device:TPU:0, one launch (start us, length us, event | category | flops | bytes accessed | tf_op | source)
XLA Modules:
  0.0 141.6 jit_solution(6117483442955089950)
XLA Ops:
  6.5 0.0 all-gather.3.cloned.1.call-start
  6.5 0.7 all-gather.3.cloned.1.call-update
  7.3 0.0 copy-start.2
  7.3 5.2 %all-to-all-start = ((bf16[8,1024,128]{2,1,0:T(8,128)(2,1)}), bf16[8,1024,128]{2,1,0:T(8,128)(2,1)S(1)}, u32[]{:S(2)}, u32[]{:S(2)}) async-start(bf16[8,1024,128]{2,1,0:T(8,128)(2,1)} %bitcast.13), calls=%async_computation | async-start | bytes 4194304 | tf_op jit(solution)/shard_map/all_to_all | solution.py:181
  12.4 0.0 copy-done.2
  12.5 0.1 reshape.42
  12.6 32.3 %all-gather.3.cloned.1.call-done = bf16[1024,512]{1,0:T(8,128)(2,1)} async-done(((bf16[128,512]{1,0:T(8,128)(2,1)}), bf16[1024,512]{1,0:T(8,128)(2,1)}) %all-gather.3.cloned.1.call-update) | async-done | bytes 1048592 | tf_op jit(solution)/shard_map/all_gather | solution.py:182
  44.8 0.0 all-to-all-done.x_ref
  44.8 0.0 copy-start.1
  44.8 1.2 copy-done.1
  46.0 2.9 %project.1.own_ref = bf16[1024,512]{1,0:T(8,128)(2,1)S(1)} custom-call(bf16[8,1024,128]{2,1,0:T(8,128)(2,1)S(1)} %all-to-all-done.x_ref, bf16[8,128,512]{2,1,0:T(8,128)(2,1)S(1)} %bitcast.10), custom_call_target="tpu_custom_call" | custom-call | tf_op jit(solution)/shard_map/project/pallas_call | solution.py:33
  49.0 0.0 copy-start
  49.0 0.7 gather_fusion
  49.7 0.3 copy-done
  50.0 53.4 %all_to_all.10 = bf16[4,4,128,512]{3,2,1,0:T(8,128)(2,1)} all-to-all(bf16[4,4,128,512]{3,2,1,0:T(8,128)(2,1)S(1)} %bitcast.11), channel_id=1, replica_groups=mesh['graph'=4,'feat'=8] {'graph'}, dimensions={0} | all-to-all | bytes 4194304 | tf_op jit(solution)/shard_map/all_to_all | solution.py:185
  103.3 31.4 %attention.1 = bf16[1024,512]{1,0:T(8,128)(2,1)} custom-call(s32[8,12]{1,0:T(8,128)} %rels_ref.1, s32[8,12]{1,0:T(8,128)} %slots_ref.1, bf16[16,128,512]{2,1,0:T(8,128)(2,1)} %bitcast.12, bf16[1024,512]{1,0:T(8,128)(2,1)} %copy-done, bf16[2,512,512]{2,1,0:T(8,128)(2,1)} %relw_ref.1, f32[2,512]{1,0:T(2,128)} %atts_ref.1, f32[2,512]{1,0:T(2,128)} %attt_ref.1, ...), custom_call_target="tpu_custom_call" | custom-call | tf_op jit(solution)/shard_map/attention/pallas_call | solution.py:146
  (2 shorter events, 0.0 us)
Async XLA Ops:
  6.5 38.3 %all-gather.3.cloned.1.call-start = ((), (), s32[]{:S(2)}) async-start(), calls=%async_computation.2 | async-start | bytes 1179648 | tf_op jit(solution)/shard_map/all_gather | solution.py:182
  7.3 5.2 %copy-start.2 = (s32[1,4,4]{2,1,0:T(4,128)S(1)}, s32[1,4,4]{2,1,0:T(4,128)}, u32[]{:S(2)}) copy-start(s32[1,4,4]{2,1,0:T(4,128)} %param.16) | copy-start | bytes 196
  7.3 37.5 %all-to-all-start = ((bf16[8,1024,128]{2,1,0:T(8,128)(2,1)}), bf16[8,1024,128]{2,1,0:T(8,128)(2,1)S(1)}, u32[]{:S(2)}, u32[]{:S(2)}) async-start(bf16[8,1024,128]{2,1,0:T(8,128)(2,1)} %bitcast.13), calls=%async_computation | async-start | bytes 4194304 | tf_op jit(solution)/shard_map/all_to_all | solution.py:181
  44.8 1.2 copy-start.1
  49.0 1.0 copy-start
Sparse Core Ops, SparseCore 0:
  9.2 35.5 all-gather.2

commit v2 on v1

--- a/solution.py
+++ b/solution.py
@@ -9,6 +9,7 @@
 from jax.sharding import PartitionSpec as P
 
 HEADS = 4
+AHEAD = 3
 LOG2E = math.log2(math.e)
 NT = (((1,), (1,)), ((), ()))
 
@@ -19,36 +20,248 @@
     return hi, lo
 
 
-def hidden_kernel(x_ref, w_ref, out_ref):
-    total = jnp.dot(x_ref[0], w_ref[0], preferred_element_type=jnp.float32)
-    for f in range(1, x_ref.shape[0]):
-        total += jnp.dot(x_ref[f], w_ref[f], preferred_element_type=jnp.float32)
-    out_ref[...] = total.astype(out_ref.dtype)
-
-
-def project(x, w):
-    feats, rows, depth = x.shape
-    width = w.shape[2]
-    tile = min(rows, 256)
+def exchange_kernel(
+    x_ref,
+    w_ref,
+    send_ref,
+    gat,
+    sends,
+    xg,
+    wg,
+    local_sem,
+    w_send,
+    w_recv,
+    x_send,
+    x_recv,
+    s_send,
+    s_recv,
+    right_send,
+    left_send,
+    z_recv,
+):
+    feats, blocks, _, depth = x_ref.shape
+    shards_g = gat.shape[0]
+    half = feats // 2
+    g = lax.axis_index("graph")
+    f = lax.axis_index("feat")
+    mesh_id = pl.DeviceIdType.MESH
+    sib = f + 1 - 2 * lax.rem(f, 2)
+
+    def feat_at(j):
+        return lax.rem(f + j, feats)
+
+    def graph_at(j):
+        return lax.rem(g + j, shards_g)
+
+    def w_rows(s):
+        return wg.at[pl.ds(pl.multiple_of(s * depth, depth), depth)]
+
+    def remote(src, dst, send_sem, recv_sem, where):
+        return pltpu.make_async_remote_copy(
+            src_ref=src,
+            dst_ref=dst,
+            send_sem=send_sem,
+            recv_sem=recv_sem,
+            device_id=where,
+            device_id_type=mesh_id,
+        )
+
+    def w_direct(j):
+        to = sib if j == 0 else feat_at(2 * j)
+        return remote(w_ref, w_rows(f), w_send.at[j], w_recv.at[f], {"feat": to})
+
+    def w_relay(j):
+        s = feat_at(2 * j)
+        return remote(w_rows(s), w_rows(s), w_send.at[half + j], w_recv.at[s], {"feat": sib})
+
+    def x_copy(j, c):
+        to = feat_at(j)
+        return remote(
+            x_ref.at[to, c], xg.at[f, c], x_send.at[j, c], x_recv.at[f, c], {"feat": to}
+        )
+
+    def x_arrival(j, c):
+        s = feat_at(j)
+        return remote(x_ref.at[s, c], xg.at[s, c], x_send.at[j, c], x_recv.at[s, c], {"feat": s})
+
+    def s_copy(j):
+        to = graph_at(j)
+        return remote(send_ref.at[to], sends.at[g], s_send.at[j], s_recv.at[g], {"graph": to})
+
+    def s_arrival(j):
+        s = graph_at(j)
+        return remote(send_ref.at[s], sends.at[s], s_send.at[j], s_recv.at[s], {"graph": s})
+
+    def z_right(o, c):
+        return remote(
+            gat.at[o, c], gat.at[o, c], right_send.at[o, c], z_recv.at[o, c], {"graph": g + 1}
+        )
+
+    def z_left(o, c):
+        return remote(
+            gat.at[o, c], gat.at[o, c], left_send.at[o, c], z_recv.at[o, c], {"graph": g - 1}
+        )
+
+    own = [
+        pltpu.make_async_copy(w_ref, w_rows(f), local_sem.at[0]),
+        pltpu.make_async_copy(x_ref.at[f], xg.at[f], local_sem.at[1]),
+        pltpu.make_async_copy(send_ref.at[g], sends.at[g], local_sem.at[2]),
+    ]
+    for copy in own:
+        copy.start()
+    barrier = pltpu.get_barrier_semaphore()
+    for j in range(1, feats):
+        pl.semaphore_signal(barrier, inc=1, device_id={"feat": feat_at(j)}, device_id_type=mesh_id)
+    for j in range(1, shards_g):
+        pl.semaphore_signal(barrier, inc=1, device_id={"graph": graph_at(j)}, device_id_type=mesh_id)
+    pl.semaphore_wait(barrier, feats + shards_g - 2)
+
+    def send_x(c):
+        for j in range(1, feats):
+            x_copy(j, c).start()
+
+    for j in range(half):
+        w_direct(j).start()
+    for c in range(min(AHEAD, blocks)):
+        send_x(c)
+    for j in range(1, shards_g):
+        s_copy(j).start()
+    for j in range(1, half):
+        w_relay(j).wait_recv()
+        w_relay(j).start()
+    for copy in own:
+        copy.wait()
+    for j in range(half):
+        s = lax.rem(sib + 2 * j, feats)
+        remote(w_ref, w_rows(s), w_send.at[0], w_recv.at[s], {"feat": sib}).wait_recv()
+
+    def forward(t):
+        for d in range(1, shards_g):
+            c = t - d
+            inside = jnp.logical_and(c >= 0, c < blocks)
+
+            @pl.when(inside & (g - d >= 0) & (g + 1 < shards_g))
+            def _():
+                z_right(g - d, c).wait_recv()
+                z_right(g - d, c).start()
+
+            @pl.when(inside & (g + d < shards_g) & (g >= 1))
+            def _():
+                z_left(g + d, c).wait_recv()
+                z_left(g + d, c).start()
+
+    def step(c, carry):
+        @pl.when(c + AHEAD < blocks)
+        def _():
+            send_x(c + AHEAD)
+
+        for j in range(1, feats):
+            x_arrival(j, c).wait_recv()
+        rows = jnp.concatenate([xg[s, c] for s in range(feats)], axis=1)
+        gat[g, c] = jnp.dot(rows, wg[...], preferred_element_type=jnp.float32).astype(gat.dtype)
+
+        @pl.when(g + 1 < shards_g)
+        def _():
+            z_right(g, c).start()
+
+        @pl.when(g >= 1)
+        def _():
+            z_left(g, c).start()
+
+        forward(c)
+        return carry
+
+    lax.fori_loop(0, blocks, step, 0)
+
+    def tail(t, carry):
+        forward(t)
+        return carry
+
+    lax.fori_loop(blocks, blocks + shards_g - 1, tail, 0)
+
+    def finish(c, carry):
+        for j in range(1, feats):
+            x_copy(j, c).wait_send()
+
+        @pl.when(g + 1 < shards_g)
+        def _():
+            z_right(g, c).wait_send()
+
+        @pl.when(g >= 1)
+        def _():
+            z_left(g, c).wait_send()
+
+        for d in range(1, shards_g):
+
+            @pl.when((g - d >= 0) & (g + 1 < shards_g))
+            def _():
+                z_right(g - d, c).wait_send()
+
+            @pl.when((g - d >= 0) & (g + 1 == shards_g))
+            def _():
+                z_left(g - d, c).wait_recv()
+
+            @pl.when((g + d < shards_g) & (g >= 1))
+            def _():
+                z_left(g + d, c).wait_send()
+
+            @pl.when((g + d < shards_g) & (g == 0))
+            def _():
+                z_right(g + d, c).wait_recv()
+
+        return carry
+
+    lax.fori_loop(0, blocks, finish, 0)
+    for j in range(half):
+        w_direct(j).wait_send()
+    for j in range(1, half):
+        w_relay(j).wait_send()
+    for j in range(1, shards_g):
+        s_copy(j).wait_send()
+        s_arrival(j).wait_recv()
+
+
+def exchange(x, w, send):
+    feats, blocks, rows, depth = x.shape
+    width = w.shape[1]
+    graphs = send.shape[0]
+    dma = pltpu.SemaphoreType.DMA
+    anywhere = pl.BlockSpec(memory_space=pl.ANY)
+    whole = pl.BlockSpec(memory_space=pltpu.VMEM)
     return pl.pallas_call(
-        hidden_kernel,
-        grid=(rows // tile,),
-        in_specs=[
-            pl.BlockSpec((feats, tile, depth), lambda i: (0, i, 0)),
-            pl.BlockSpec((feats, depth, width), lambda i: (0, 0, 0)),
+        exchange_kernel,
+        in_specs=[anywhere, anywhere, whole],
+        out_specs=[whole, whole],
+        out_shape=[
+            jax.ShapeDtypeStruct((graphs, blocks, rows, width), jnp.bfloat16),
+            jax.ShapeDtypeStruct(send.shape, jnp.int32),
         ],
-        out_specs=pl.BlockSpec((tile, width), lambda i: (i, 0)),
-        out_shape=jax.ShapeDtypeStruct((rows, width), jnp.bfloat16),
-        compiler_params=pltpu.CompilerParams(vmem_limit_bytes=40 << 20),
-        name="project",
-    )(x, w)
+        scratch_shapes=[
+            pltpu.VMEM((feats, blocks, rows, depth), jnp.bfloat16),
+            pltpu.VMEM((feats * depth, width), jnp.bfloat16),
+            dma((3,)),
+            dma((feats,)),
+            dma((feats,)),
+            dma((feats, blocks)),
+            dma((feats, blocks)),
+            dma((graphs,)),
+            dma((graphs,)),
+            dma((graphs, blocks)),
+            dma((graphs, blocks)),
+            dma((graphs, blocks)),
+        ],
+        compiler_params=pltpu.CompilerParams(
+            collective_id=0, has_side_effects=True, vmem_limit_bytes=40 << 20
+        ),
+        name="exchange",
+    )(x, w, send)
 
 
 def attention_kernel(
     rels_ref,
     slots_ref,
+    sends_ref,
     front_ref,
-    own_ref,
     relw_ref,
     atts_ref,
     attt_ref,
@@ -63,9 +276,9 @@
     bias,
     weights,
 ):
-    slots = front_ref.shape[0]
-    rows = front_ref.shape[1]
-    width = front_ref.shape[2]
+    graphs, blocks, rows, width = front_ref.shape
+    cap = values.shape[0] // (relw_ref.shape[0] * graphs)
+    slots = graphs * cap
     hw = width // HEADS
     relations = relw_ref.shape[0]
     lists = mask_ref.shape[1]
@@ -83,16 +296,20 @@
             ]
             att = jnp.concatenate(parts, axis=0).astype(jnp.bfloat16)
 
-            def one_slot(s, carry):
-                v = jnp.dot(
-                    front_ref[s], relw_ref[r], preferred_element_type=jnp.float32
-                ).astype(jnp.bfloat16)
-                values[r * slots + s] = v
+            def one_sender(q, carry):
+                taken = jnp.concatenate(
+                    [front_ref[q, sends_ref[q, 0, c]] for c in range(cap)], axis=0
+                )
+                v = jnp.dot(taken, relw_ref[r], preferred_element_type=jnp.float32)
+                v = v.astype(jnp.bfloat16)
                 both = lax.dot_general(att, v, NT, preferred_element_type=jnp.float32)
-                scores[r * slots + s] = both[:8] + both[8:]
+                both = both[:8] + both[8:]
+                for c in range(cap):
+                    values[r * slots + q * cap + c] = v[c * rows : (c + 1) * rows]
+                    scores[r * slots + q * cap + c] = both[:, c * rows : (c + 1) * rows]
                 return carry
 
-            lax.fori_loop(0, slots, one_slot, 0)
+            lax.fori_loop(0, graphs, one_sender, 0)
             hi, lo = split_bf16(attt_ref[r : r + 1, :] * LOG2E)
             for n, part in enumerate((hi, lo)):
                 tatt[n, r * rows : (r + 1) * rows, :] = jnp.broadcast_to(
@@ -100,6 +317,7 @@
                 ).astype(jnp.bfloat16)
         stack[:, :, hw:] = jnp.ones((HEADS, lists * rows, hw), jnp.bfloat16)
 
+    mine = front_ref.at[lax.axis_index("graph"), b]
     index = []
     for k in range(lists):
         rel = rels_ref[b, k]
@@ -111,7 +329,7 @@
         bias[k] = jnp.where(mask_ref[0, k] > 0, 0.0, -jnp.inf)
     for h in range(HEADS):
         cols = slice(h * hw, (h + 1) * hw)
-        own = own_ref[:, cols]
+        own = mine[:, cols]
         both = lax.dot_general(
             own, tatt[0, :, cols], NT, preferred_element_type=jnp.float32
         ) + lax.dot_general(own, tatt[1, :, cols], NT, preferred_element_type=jnp.float32)
@@ -136,8 +354,9 @@
         ).astype(out_ref.dtype)
 
 
-def attention(rels, slots, front, hidden, relw, atts, attt, mask):
-    count, rows, width = front.shape
+def attention(rels, slots, sends, front, cap, relw, atts, attt, mask):
+    graphs, _, rows, width = front.shape
+    count = graphs * cap
     blocks, lists = mask.shape[:2]
     relations = relw.shape[0]
     hw = width // HEADS
@@ -149,8 +368,8 @@
         in_specs=[
             smem,
             smem,
+            smem,
             whole,
-            pl.BlockSpec((rows, width), lambda b: (b, 0)),
             whole,
             whole,
             whole,
@@ -170,21 +389,17 @@
         ],
         compiler_params=pltpu.CompilerParams(vmem_limit_bytes=56 << 20),
         name="attention",
-    )(rels, slots, front, hidden, relw, atts, attt, mask)
+    )(rels, slots, sends, front, relw, atts, attt, mask)
 
 
 def shards(x, w, relw, atts, attt, mask, rels, send, slots):
     rows = mask.shape[-1]
     blocks = mask.shape[0]
-    feats = x.shape[0] // (blocks * rows)
-    x = x.reshape(feats, blocks * rows, x.shape[1])
-    x = lax.all_to_all(x, "feat", split_axis=0, concat_axis=0, tiled=True)
-    w = lax.all_gather(w, "feat", axis=0)
-    hidden = project(x, w)
-    out = hidden.reshape(blocks, rows, -1)[send[0]]
-    front = lax.all_to_all(out, "graph", split_axis=0, concat_axis=0, tiled=True)
-    front = front.reshape((-1,) + front.shape[2:])
-    return attention(rels, slots, front, hidden, relw, atts, attt, mask)
+    cap = send.shape[2]
+    x = x.reshape(-1, blocks, rows, x.shape[1])
+    tiles = jnp.pad(send[0][:, None, :], ((0, 0), (0, 7), (0, 128 - cap)))
+    front, sends = exchange(x, w, tiles)
+    return attention(rels, slots, sends, front, cap, relw, atts, attt, mask)
 
 
 def solution(mesh):

time: 142 us -> 119 us (0.84)
  Pallas kernels: 34.3 us -> 113 us
  blocking collectives: 53.4 us -> 0 us
  waiting for transfers between devices: 33 us -> 0 us
  between operations: 13.4 us -> 0.02 us
  starting transfers between devices: 5.18 us -> 0 us
  local copies, waits for them, and re-layouts: 2.28 us -> 5.71 us
    pallas_call x2, Pallas kernels: 34.3 us -> 113 us  [the longest x1 87.7 us: exchange(): pl.pallas_call(exchange_kernel, in_specs=[anywhere, anywhere, whole], out...]
    all_to_all x1 -> x0, blocking collectives: 53.4 us -> none  [shards(): lax.all_to_all(out, 'graph', split_axis=0, concat_axis=0, tiled=True)]
    all_gather x1 -> x0, waiting for transfers between devices: 32.3 us -> none  [shards(): w = lax.all_gather(w, 'feat', axis=0)]
    all_to_all x1 -> x0, starting transfers between devices: 5.18 us -> none  [shards(): x = lax.all_to_all(x, 'feat', split_axis=0, concat_axis=0, tiled=True)]
    unnamed x6 -> x8, local copies, waits for them, and re-layouts: 1.52 us -> 5.02 us
  transfers between devices with their start and end apart: 2 -> 0, of which waited for: 1 -> 0; matrix products, arithmetic and copies ran while one was open for 0% -> 0% of each run, Pallas kernels for 0% -> 0%
where the time goes in v2:
time: 119 us
  Pallas kernels  113 us (95%)
  local copies, waits for them, and re-layouts  5.71 us (5%)
    pallas_call x1, Pallas kernels, exchange(): pl.pallas_call(exchange_kernel, in_specs=[anywhere, anywhere, whole], out...  87.7 us
    pallas_call x1, Pallas kernels, attention(): pl.pallas_call(attention_kernel, grid=(blocks,), in_specs=[smem, smem, sm...  25.5 us
    unnamed x8, local copies, waits for them, and re-layouts  5.02 us

profile of v2, /device:TPU:0, one launch (start us, length us, event | category | flops | bytes accessed | tf_op | source)
XLA Modules:
  0.0 118.9 jit_solution(8715902396505423059)
XLA Ops:
  0.0 0.7 pad.4.send_ref
  0.7 0.0 copy-start.1
  0.7 1.6 %copy-done.1 = bf16[8192,128]{1,0:T(8,128)(2,1)S(1)} copy-done((bf16[8192,128]{1,0:T(8,128)(2,1)S(1)}, bf16[8192,128]{1,0:T(8,128)(2,1)}, u32[]{:S(2)}) %copy-start.1) | copy-done | bytes 2097176
  2.3 0.0 copy-start.2
  2.3 0.9 copy-done.2
  3.2 87.7 %exchange.1 = (bf16[4,8,128,512]{3,2,1,0:T(8,128)(2,1)S(1)}, s32[4,8,128]{2,1,0:T(8,128)S(1)}) custom-call(bf16[8,8,128,128]{3,2,1,0:T(8,128)(2,1)S(1)} %bitcast.4, bf16[128,512]{1,0:T(8,128)(2,1)S(1)} %copy-done.2, s32[4,8,128]{2,1,0:T(8,128)S(1)} %pad.4.send_ref), custom_call_target="tpu_custom_call" | custom-call | tf_op jit(solution)/shard_map/exchange/pallas_call | solution.py:231
  90.9 0.0 copy-start
  90.9 1.9 %copy-done = bf16[4,8,128,512]{3,2,1,0:T(8,128)(2,1)} copy-done((bf16[4,8,128,512]{3,2,1,0:T(8,128)(2,1)}, bf16[4,8,128,512]{3,2,1,0:T(8,128)(2,1)S(1)}, u32[]{:S(2)}) %copy-start) | copy-done | bytes 4194328
  92.8 0.0 copy-start.3
  92.8 0.6 copy-done.3
  93.4 25.5 %attention.1 = bf16[1024,512]{1,0:T(8,128)(2,1)} custom-call(s32[8,12]{1,0:T(8,128)} %rels_ref.1, s32[8,12]{1,0:T(8,128)} %slots_ref.1, s32[4,8,128]{2,1,0:T(8,128)} %copy-done.3, bf16[4,8,128,512]{3,2,1,0:T(8,128)(2,1)} %copy-done, bf16[2,512,512]{2,1,0:T(8,128)(2,1)} %relw_ref.1, f32[2,512]{1,0:T(2,128)} %atts_ref.1, f32[2,512]{1,0:T(2,128)} %attt_ref.1, ...), custom_call_target="tpu_custom_call" | custom-call | tf_op jit(solution)/shard_map/attention/pallas_call | solution.py:365
Async XLA Ops:
  0.7 1.6 %copy-start.1 = (bf16[8192,128]{1,0:T(8,128)(2,1)S(1)}, bf16[8192,128]{1,0:T(8,128)(2,1)}, u32[]{:S(2)}) copy-start(bf16[8192,128]{1,0:T(8,128)(2,1)} %param.9) | copy-start | bytes 6291460
  2.3 0.9 copy-start.2
  90.9 1.9 %copy-start = (bf16[4,8,128,512]{3,2,1,0:T(8,128)(2,1)}, bf16[4,8,128,512]{3,2,1,0:T(8,128)(2,1)S(1)}, u32[]{:S(2)}) copy-start(bf16[4,8,128,512]{3,2,1,0:T(8,128)(2,1)S(1)} %get-tuple-element.8.front_ref) | copy-start | bytes 12582916
  92.8 0.6 copy-start.3

commit v3 on v0

v3 whole, which is shorter than its diff:
```python
import math

import jax
import jax.numpy as jnp
from jax import lax
from jax.experimental import pallas as pl
from jax.experimental.pallas import tpu as pltpu
from jax.sharding import PartitionSpec as P

HEADS = 4
CHUNKS = 2
LOG2E = math.log2(math.e)
NT = (((1,), (1,)), ((), ()))


def split_bf16(x):
    hi = x.astype(jnp.bfloat16)
    lo = (x - hi.astype(jnp.float32)).astype(jnp.bfloat16)
    return hi, lo


def layer_kernel(
    send_ref,
    rels_ref,
    slots_ref,
    x_ref,
    w_ref,
    relw_ref,
    atts_ref,
    attt_ref,
    mask_ref,
    out_ref,
    xg,
    wg,
    hid,
    stage,
    front,
    values,
    scores,
    satt,
    tatt,
    target,
    stack,
    raws,
    weights,
    live,
    bias,
    local_sem,
    w_send,
    w_recv,
    x_send,
    x_recv,
    z_send,
    z_recv,
):
    feats, blocks, rows, depth = x_ref.shape
    graphs, cap = send_ref.shape
    width = w_ref.shape[1]
    relations = relw_ref.shape[0]
    lists = mask_ref.shape[1]
    slots = graphs * cap
    hw = width // HEADS
    half = feats // 2
    part = blocks // CHUNKS
    g = lax.axis_index("graph")
    f = lax.axis_index("feat")
    mesh_id = pl.DeviceIdType.MESH
    sib = f + 1 - 2 * lax.rem(f, 2)

    def feat_at(j):
        return lax.rem(f + j, feats)

    def graph_at(j):
        place, bit = 0, 1
        while bit < graphs:
            place = place + bit * ((g // bit + j // bit) % 2)
            bit *= 2
        return place

    def w_rows(s):
        return wg.at[pl.ds(pl.multiple_of(s * depth, depth), depth)]

    def remote(src, dst, send_sem, recv_sem, where):
        return pltpu.make_async_remote_copy(
            src_ref=src,
            dst_ref=dst,
            send_sem=send_sem,
            recv_sem=recv_sem,
            device_id=where,
            device_id_type=mesh_id,
        )

    def w_direct(j):
        to = sib if j == 0 else feat_at(2 * j)
        return remote(w_ref, w_rows(f), w_send.at[j], w_recv.at[f], {"feat": to})

    def w_relay(j):
        s = feat_at(2 * j)
        return remote(w_rows(s), w_rows(s), w_send.at[half + j], w_recv.at[s], {"feat": sib})

    def piece(c):
        return pl.ds(c * part, part)

    def x_copy(j, c):
        to = feat_at(j)
        return remote(
            x_ref.at[to, piece(c)],
            xg.at[f, piece(c)],
            x_send.at[j, c],
            x_recv.at[f, c],
            {"feat": to},
        )

    def x_arrival(j, c):
        s = feat_at(j)
        return remote(
            x_ref.at[s, piece(c)],
            xg.at[s, piece(c)],
            x_send.at[j, c],
            x_recv.at[s, c],
            {"feat": s},
        )

    def z_copy(j, c):
        to = graph_at(j)
        return remote(
            stage.at[j, c], front.at[g, c], z_send.at[j, c], z_recv.at[g, c], {"graph": to}
        )

    def z_arrival(j, c):
        q = graph_at(j)
        return remote(
            stage.at[j, c], front.at[q, c], z_send.at[j, c], z_recv.at[q, c], {"graph": q}
        )

    own = [
        pltpu.make_async_copy(w_ref, w_rows(f), local_sem.at[0]),
        pltpu.make_async_copy(x_ref.at[f], xg.at[f], local_sem.at[1]),
    ]
    masks = pltpu.make_async_copy(mask_ref, live, local_sem.at[2])
    for copy in own:
        copy.start()
    barrier = pltpu.get_barrier_semaphore()
    for j in range(1, feats):
        pl.semaphore_signal(barrier, inc=1, device_id={"feat": feat_at(j)}, device_id_type=mesh_id)
    for j in range(1, graphs):
        pl.semaphore_signal(barrier, inc=1, device_id={"graph": graph_at(j)}, device_id_type=mesh_id)
    pl.semaphore_wait(barrier, feats + graphs - 2)

    for j in range(half):
        w_direct(j).start()
    for c in range(CHUNKS):
        for j in range(1, feats):
            x_copy(j, c).start()
    masks.start()

    head_of = lax.broadcasted_iota(jnp.int32, (8, width), 1) // hw
    row_of = lax.broadcasted_iota(jnp.int32, (8, width), 0)
    for r in range(relations):
        parts = [
            jnp.where(head_of == row_of, half_att.astype(jnp.float32), 0.0)
            for half_att in split_bf16(atts_ref[r : r + 1, :] * LOG2E)
        ]
        satt[r] = jnp.concatenate(parts, axis=0).astype(jnp.bfloat16)
        for n, half_att in enumerate(split_bf16(attt_ref[r : r + 1, :] * LOG2E)):
            tatt[n, r * rows : (r + 1) * rows, :] = jnp.broadcast_to(
                half_att.astype(jnp.float32), (rows, width)
            ).astype(jnp.bfloat16)
    stack[:, :, hw:] = jnp.ones((HEADS, lists * rows, hw), jnp.bfloat16)

    for j in range(1, half):
        w_relay(j).wait_recv()
        w_relay(j).start()
    for copy in own:
        copy.wait()
    masks.wait()

    def make_bias(b, carry):
        bias[b] = jnp.where(live[b] > 0, 0.0, -jnp.inf)
        return carry

    lax.fori_loop(0, blocks, make_bias, 0)
    for j in range(half):
        s = lax.rem(sib + 2 * j, feats)
        remote(w_ref, w_rows(s), w_send.at[0], w_recv.at[s], {"feat": sib}).wait_recv()

    def project(c, carry):
        for j in range(1, feats):
            x_arrival(j, c).wait_recv()
        taken = jnp.concatenate(
            [xg[s, piece(c)].reshape(part * rows, depth) for s in range(feats)], axis=1
        )
        made = jnp.dot(taken, wg[...], preferred_element_type=jnp.float32)
        hid[piece(c)] = made.astype(hid.dtype).reshape(part, rows, width)
        return carry

    lax.fori_loop(0, CHUNKS, project, 0)

    def send_frontier(n, carry):
        j = graphs - 1 - n
        to = graph_at(j)
        for c in range(cap):
            stage[j, c] = hid[send_ref[to, c]]
            z_copy(j, c).start()
        return carry

    lax.fori_loop(0, graphs - 1, send_frontier, 0)
    for c in range(cap):
        front[g, c] = hid[send_ref[g, c]]

    def score_targets(c, carry):
        mine = hid[piece(c)].reshape(part * rows, width)
        for h in range(HEADS):
            cols = slice(h * hw, (h + 1) * hw)
            both = lax.dot_general(
                mine[:, cols], tatt[0, :, cols], NT, preferred_element_type=jnp.float32
            ) + lax.dot_general(
                mine[:, cols], tatt[1, :, cols], NT, preferred_element_type=jnp.float32
            )
            for r in range(relations):
                target[h, r, piece(c)] = both[:, r * rows : (r + 1) * rows].reshape(
                    part, rows, rows
                )
        return carry

    def transform(j):
        q = graph_at(j)
        taken = front[q].reshape(cap * rows, width)

        def relation(r, carry):
            v = jnp.dot(taken, relw_ref[r], preferred_element_type=jnp.float32)
            v = v.astype(jnp.bfloat16)
            both = lax.dot_general(satt[r], v, NT, preferred_element_type=jnp.float32)
            both = both[:8] + both[8:]
            for c in range(cap):
                values[r * slots + q * cap + c] = v[c * rows : (c + 1) * rows]
                scores[r * slots + q * cap + c] = both[:, c * rows : (c + 1) * rows]
            return carry

        lax.fori_loop(0, relations, relation, 0)

    transform(0)
    lax.fori_loop(0, CHUNKS, score_targets, 0)

    def receive(j, carry):
        for c in range(cap):
            z_arrival(j, c).wait_recv()
        transform(j)
        return carry

    lax.fori_loop(1, graphs, receive, 0)

    def attend(b, carry):
        index = []
        for k in range(lists):
            rel = rels_ref[b, k]
            index.append((rel, rel * slots + slots_ref[b, k]))
        for k in range(lists):
            v = values[index[k][1]]
            for h in range(HEADS):
                stack[h, k * rows : (k + 1) * rows, :hw] = v[:, h * hw : (h + 1) * hw]
        for h in range(HEADS):
            top = None
            for k in range(lists):
                rel, place = index[k]
                raw = (target[h, rel, b] + scores[place, h : h + 1, :]) + bias[b, k]
                raws[h, k] = raw
                top = raw if top is None else jnp.maximum(top, raw)
            top = jnp.max(top, axis=1, keepdims=True)
            top = jnp.broadcast_to(jnp.maximum(top, 0.2 * top), (rows, rows))
            for k in range(lists):
                raw = raws[h, k]
                prob = jnp.exp2(jnp.maximum(raw, 0.2 * raw) - top)
                weights[h, :, k * rows : (k + 1) * rows] = prob.astype(jnp.bfloat16)
        for h in range(HEADS):
            cols = slice(h * hw, (h + 1) * hw)
            summed = jnp.dot(weights[h], stack[h], preferred_element_type=jnp.float32)
            mixed = summed[:, :hw] / summed[:, hw:] + hid[b, :, cols].astype(jnp.float32)
            out_ref[b, :, cols] = jnp.where(
                mixed > 0, mixed, jnp.exp(jnp.minimum(mixed, 0.0)) - 1.0
            ).astype(out_ref.dtype)
        return carry

    lax.fori_loop(0, blocks, attend, 0)

    for c in range(CHUNKS):
        for j in range(1, feats):
            x_copy(j, c).wait_send()
    for j in range(half):
        w_direct(j).wait_send()
    for j in range(1, half):
        w_relay(j).wait_send()
    for j in range(1, graphs):
        for c in range(cap):
            z_copy(j, c).wait_send()


def layer(send, rels, slots, x, w, relw, atts, attt, mask):
    feats, blocks, rows, depth = x.shape
    width = w.shape[1]
    graphs, cap = send.shape
    lists = mask.shape[1]
    relations = relw.shape[0]
    count = relations * graphs * cap
    hw = width // HEADS
    dma = pltpu.SemaphoreType.DMA
    anywhere = pl.BlockSpec(memory_space=pl.ANY)
    whole = pl.BlockSpec(memory_space=pltpu.VMEM)
    smem = pl.BlockSpec(memory_space=pltpu.SMEM)
    bf16, f32 = jnp.bfloat16, jnp.float32
    return pl.pallas_call(
        layer_kernel,
        in_specs=[smem, smem, smem, anywhere, anywhere, whole, whole, whole, anywhere],
        out_specs=whole,
        out_shape=jax.ShapeDtypeStruct((blocks, rows, width), bf16),
        scratch_shapes=[
            pltpu.VMEM((feats, blocks, rows, depth), bf16),
            pltpu.VMEM((feats * depth, width), bf16),
            pltpu.VMEM((blocks, rows, width), bf16),
            pltpu.VMEM((graphs, cap, rows, width), bf16),
            pltpu.VMEM((graphs, cap, rows, width), bf16),
            pltpu.VMEM((count, rows, width), bf16),
            pltpu.VMEM((count, 8, rows), f32),
            pltpu.VMEM((relations, 16, width), bf16),
            pltpu.VMEM((2, relations * rows, width), bf16),
            pltpu.VMEM((HEADS, relations, blocks, rows, rows), f32),
            pltpu.VMEM((HEADS, lists * rows, 2 * hw), bf16),
            pltpu.VMEM((HEADS, lists, rows, rows), f32),
            pltpu.VMEM((HEADS, rows, lists * rows), bf16),
            pltpu.VMEM(mask.shape, jnp.int32),
            pltpu.VMEM(mask.shape, f32),
            dma((3,)),
            dma((feats,)),
            dma((feats,)),
            dma((feats, CHUNKS)),
            dma((feats, CHUNKS)),
            dma((graphs, cap)),
            dma((graphs, cap)),
        ],
        compiler_params=pltpu.CompilerParams(
            collective_id=0, has_side_effects=True, vmem_limit_bytes=58 << 20
        ),
        name="layer",
    )(send, rels, slots, x, w, relw, atts, attt, mask)


def shards(x, w, relw, atts, attt, mask, rels, send, slots):
    rows = mask.shape[-1]
    blocks = mask.shape[0]
    x = x.reshape(-1, blocks, rows, x.shape[1])
    out = layer(send[0], rels, slots, x, w, relw, atts, attt, mask)
    return out.reshape(blocks * rows, -1)


def solution(mesh):
    placed = (
        P("graph", "feat"),
        P("feat", None),
        P(),
        P(),
        P(),
        P(("graph", "feat"), None, None, None),
        P(("graph", "feat"), None),
        P(("graph", "feat"), None, None),
        P(("graph", "feat"), None),
    )
    return jax.shard_map(
        shards, mesh=mesh, in_specs=placed, out_specs=P(("graph", "feat"), None), check_vma=False
    )
```

time: 348 us -> 102 us (0.29)
  waiting for transfers between devices: 161 us -> 0 us
  Pallas kernels: 0 us -> 99.4 us
  local copies, waits for them, and re-layouts: 76.7 us -> 2.26 us
  other arithmetic: 54.5 us -> 0 us
  matrix products: 33.9 us -> 0 us
  between operations: 13.4 us -> 0.01 us
  starting transfers between devices: 4.74 us -> 0 us
    reduce_scatter x1 -> x0, waiting for transfers between devices: 118 us -> none  [shards(): lax.psum_scatter(jnp.dot(node_features, proj_weight, preferred_element_ty...]
    pallas_call x0 -> x1, Pallas kernels: none -> 99.4 us  [layer(): pl.pallas_call(layer_kernel, in_specs=[smem, smem, smem, anywhere, anywhe...]
    all_to_all x1 -> x0, waiting for transfers between devices: 43.4 us -> none  [shards(): lax.all_to_all(outgoing, 'graph', split_axis=0, concat_axis=0, tiled=True)]
    gather x25 -> x0, local copies, waits for them, and re-layouts: 34.6 us -> none  [the longest x8 22.7 us: one_block(): chosen = values[slots, rels]]
    dot_general x10 -> x0, matrix products: 33.9 us -> none  [the longest x8 16.9 us: attend(): jnp.einsum('hix,xhd->hid', weights, stacked, preferred_element_type=jnp.f...]
    convert_element_type x17 -> x0, other arithmetic: 19.6 us -> none  [the longest x8 16.8 us: attend(): prob.astype(jnp.bfloat16)]
    reduce_sum x10 -> x0, other arithmetic: 19.1 us -> none  [the longest x8 9.97 us: attend(): total = jnp.sum(prob, axis=(2, 3))]
    reshape x9 -> x0, local copies, waits for them, and re-layouts: 13.3 us -> none  [the longest x1 9.92 us: shards(): transform_values.astype(jnp.float32)]
  transfers between devices with their start and end apart: 2 -> 0, of which waited for: 2 -> 0; matrix products, arithmetic and copies ran while one was open for 1% -> 0% of each run, Pallas kernels for 0% -> 0%
where the time goes in v3:
time: 102 us
  Pallas kernels  99.4 us (97%)
  local copies, waits for them, and re-layouts  2.26 us (2%)
    pallas_call x1, Pallas kernels, layer(): pl.pallas_call(layer_kernel, in_specs=[smem, smem, smem, anywhere, anywhe...  99.4 us
    unnamed x1, local copies, waits for them, and re-layouts  2.26 us

profile of v3, /device:TPU:0, one launch (start us, length us, event | category | flops | bytes accessed | tf_op | source)
XLA Modules:
  0.0 101.6 jit_solution(13482697201714240309)
XLA Ops:
  0.0 99.4 %layer.1 = bf16[8,128,512]{2,1,0:T(8,128)(2,1)} custom-call(s32[4,4]{1,0:T(4,128)} %bitcast.5, s32[8,12]{1,0:T(8,128)} %rels_ref.1, s32[8,12]{1,0:T(8,128)} %slots_ref.1, bf16[8,8,128,128]{3,2,1,0:T(8,128)(2,1)} %bitcast.4, bf16[128,512]{1,0:T(8,128)(2,1)} %w_ref.1, bf16[2,512,512]{2,1,0:T(8,128)(2,1)} %relw_ref.1, f32[2,512]{1,0:T(2,128)} %atts_ref.1, ...), custom_call_target="tpu_custom_call" | custom-call | tf_op jit(solution)/shard_map/layer/pallas_call | solution.py:311
  99.4 2.3 %copy.11 = bf16[1024,512]{1,0:T(8,128)(2,1)} copy(bf16[1024,512]{1,0:T(8,128)(2,1)} %bitcast.3) | data formatting | bytes 2097152

commit v4 on v3

--- a/solution.py
+++ b/solution.py
@@ -8,7 +8,6 @@
 from jax.sharding import PartitionSpec as P
 
 HEADS = 4
-CHUNKS = 2
 LOG2E = math.log2(math.e)
 NT = (((1,), (1,)), ((), ()))
 
@@ -21,6 +20,7 @@
 
 def layer_kernel(
     send_ref,
+    tiles_ref,
     rels_ref,
     slots_ref,
     x_ref,
@@ -30,6 +30,11 @@
     attt_ref,
     mask_ref,
     out_ref,
+    lists_got,
+    lists_smem,
+    spot,
+    xin,
+    xst,
     xg,
     wg,
     hid,
@@ -46,6 +51,8 @@
     live,
     bias,
     local_sem,
+    l_send,
+    l_recv,
     w_send,
     w_recv,
     x_send,
@@ -60,22 +67,42 @@
     lists = mask_ref.shape[1]
     slots = graphs * cap
     hw = width // HEADS
-    half = feats // 2
-    part = blocks // CHUNKS
+    parts = ((0, cap), (cap, blocks - cap))
     g = lax.axis_index("graph")
     f = lax.axis_index("feat")
     mesh_id = pl.DeviceIdType.MESH
-    sib = f + 1 - 2 * lax.rem(f, 2)
-
-    def feat_at(j):
-        return lax.rem(f + j, feats)
-
-    def graph_at(j):
+    parity = lax.rem(f, 2)
+
+    def flip(index, bits, size):
         place, bit = 0, 1
-        while bit < graphs:
-            place = place + bit * ((g // bit + j // bit) % 2)
+        while bit < size:
+            place = place + bit * ((index // bit + bits // bit) % 2)
             bit *= 2
         return place
+
+    if feats == 8:
+        even, odd = (2, 4, 6, 3, 5, 7, 1), (4, 2, 7, 5, 3, 6, 1)
+    else:
+        even = odd = tuple(range(1, feats))
+    pairs = tuple(m for m in range(2, feats, 2))
+    turns = tuple(pairs[1:2] + pairs[:1] + pairs[2:])
+
+    def feat_at(n):
+        return flip(f, even[n] + parity * (odd[n] - even[n]), feats)
+
+    def same_core(n):
+        return flip(f, pairs[n] + parity * (turns[n] - pairs[n]), feats)
+
+    sib = f + 1 - 2 * parity
+    others = range(feats - 1)
+    chips = range(len(pairs))
+    inner = jnp.logical_and(g > 0, g < graphs - 1)
+
+    def graph_at(j):
+        return flip(g, j, graphs)
+
+    def order(n):
+        return graphs - 1 - n + jnp.where(inner, 1 if n else 2 - graphs, 0)
 
     def w_rows(s):
         return wg.at[pl.ds(pl.multiple_of(s * depth, depth), depth)]
@@ -90,37 +117,57 @@
             device_id_type=mesh_id,
         )
 
-    def w_direct(j):
-        to = sib if j == 0 else feat_at(2 * j)
-        return remote(w_ref, w_rows(f), w_send.at[j], w_recv.at[f], {"feat": to})
-
-    def w_relay(j):
-        s = feat_at(2 * j)
-        return remote(w_rows(s), w_rows(s), w_send.at[half + j], w_recv.at[s], {"feat": sib})
+    def w_direct(n):
+        to = same_core(n) if n < len(pairs) else sib
+        return remote(w_ref, w_rows(f), w_send.at[n], w_recv.at[f], {"feat": to})
+
+    def w_relay(n):
+        s = same_core(n)
+        return remote(w_rows(s), w_rows(s), w_send.at[feats + n], w_recv.at[s], {"feat": sib})
 
     def piece(c):
-        return pl.ds(c * part, part)
-
-    def x_copy(j, c):
-        to = feat_at(j)
-        return remote(
-            x_ref.at[to, piece(c)],
+        return pl.ds(*parts[c])
+
+    def x_copy(n, c):
+        to = feat_at(n)
+        return remote(
+            xst.at[to, piece(c)],
             xg.at[f, piece(c)],
-            x_send.at[j, c],
+            x_send.at[n, c],
             x_recv.at[f, c],
             {"feat": to},
         )
 
-    def x_arrival(j, c):
-        s = feat_at(j)
-        return remote(
-            x_ref.at[s, piece(c)],
+    def x_arrival(n, c):
+        s = feat_at(n)
+        return remote(
+            xst.at[s, piece(c)],
             xg.at[s, piece(c)],
-            x_send.at[j, c],
+            x_send.at[n, c],
             x_recv.at[s, c],
             {"feat": s},
         )
 
+    first = graph_at(order(0))
+
+    def l_copy(n):
+        to = feat_at(n)
+        return remote(
+            tiles_ref.at[first], lists_got.at[f], l_send.at[n], l_recv.at[f], {"feat": to}
+        )
+
+    def l_arrival(n):
+        s = feat_at(n)
+        return remote(
+            tiles_ref.at[first], lists_got.at[s], l_send.at[n], l_recv.at[s], {"feat": s}
+        )
+
+    def z_first(c):
+        j = order(0)
+        return remote(
+            hid.at[c], front.at[g, c], z_send.at[j, c], z_recv.at[g, c], {"graph": first}
+        )
+
     def z_copy(j, c):
         to = graph_at(j)
         return remote(
@@ -135,44 +182,86 @@
 
     own = [
         pltpu.make_async_copy(w_ref, w_rows(f), local_sem.at[0]),
-        pltpu.make_async_copy(x_ref.at[f], xg.at[f], local_sem.at[1]),
+        pltpu.make_async_copy(x_ref, xin, local_sem.at[1]),
+        pltpu.make_async_copy(tiles_ref.at[first], lists_got.at[f], local_sem.at[2]),
     ]
-    masks = pltpu.make_async_copy(mask_ref, live, local_sem.at[2])
+    masks = pltpu.make_async_copy(mask_ref, live, local_sem.at[3])
     for copy in own:
         copy.start()
     barrier = pltpu.get_barrier_semaphore()
-    for j in range(1, feats):
-        pl.semaphore_signal(barrier, inc=1, device_id={"feat": feat_at(j)}, device_id_type=mesh_id)
+    for n in others:
+        pl.semaphore_signal(barrier, inc=1, device_id={"feat": feat_at(n)}, device_id_type=mesh_id)
     for j in range(1, graphs):
         pl.semaphore_signal(barrier, inc=1, device_id={"graph": graph_at(j)}, device_id_type=mesh_id)
     pl.semaphore_wait(barrier, feats + graphs - 2)
 
-    for j in range(half):
-        w_direct(j).start()
-    for c in range(CHUNKS):
-        for j in range(1, feats):
-            x_copy(j, c).start()
+    for n in others:
+        l_copy(n).start()
+    for n in range(len(pairs) + 1):
+        w_direct(n).start()
+    for copy in own:
+        copy.wait()
+    for n in others:
+        l_arrival(n).wait_recv()
+    to_smem = pltpu.make_async_copy(lists_got, lists_smem, local_sem.at[4])
+    to_smem.start()
+    to_smem.wait()
+
+    def unlisted(s, block):
+        used = 0
+        for c in range(cap):
+            used = used + jnp.where(lists_smem[s, 0, c] == block, 1, 0)
+        return 1 - jnp.minimum(used, 1)
+
+    def fill(s, c):
+        if c == 0:
+            for t in range(cap):
+                xst[s, t] = xin[s, lists_smem[s, 0, t]]
+        else:
+            free = [unlisted(s, block) for block in range(blocks)]
+            for t in range(blocks - cap):
+                found, seen = 0, 0
+                for block in range(blocks):
+                    hit = jnp.where(seen == t, free[block], 0)
+                    found = found + hit * block
+                    seen = seen + free[block]
+                xst[s, cap + t] = xin[s, jnp.minimum(found, blocks - 1)]
+
+    for n in others:
+        fill(feat_at(n), 0)
+        x_copy(n, 0).start()
+    for n in chips:
+        w_relay(n).wait_recv()
+        w_relay(n).start()
+    for n in others:
+        fill(feat_at(n), 1)
+        x_copy(n, 1).start()
+    for c in range(2):
+        fill(f, c)
+    seen = 0
+    for block in range(blocks):
+        place = 0
+        for c in range(cap):
+            place = place + jnp.where(lists_smem[f, 0, c] == block, c, 0)
+        free = unlisted(f, block)
+        spot[block] = jnp.minimum(place + free * (cap + seen), blocks - 1)
+        seen = seen + free
     masks.start()
 
     head_of = lax.broadcasted_iota(jnp.int32, (8, width), 1) // hw
     row_of = lax.broadcasted_iota(jnp.int32, (8, width), 0)
     for r in range(relations):
-        parts = [
+        halves = [
             jnp.where(head_of == row_of, half_att.astype(jnp.float32), 0.0)
             for half_att in split_bf16(atts_ref[r : r + 1, :] * LOG2E)
         ]
-        satt[r] = jnp.concatenate(parts, axis=0).astype(jnp.bfloat16)
+        satt[r] = jnp.concatenate(halves, axis=0).astype(jnp.bfloat16)
         for n, half_att in enumerate(split_bf16(attt_ref[r : r + 1, :] * LOG2E)):
             tatt[n, r * rows : (r + 1) * rows, :] = jnp.broadcast_to(
                 half_att.astype(jnp.float32), (rows, width)
             ).astype(jnp.bfloat16)
     stack[:, :, hw:] = jnp.ones((HEADS, lists * rows, hw), jnp.bfloat16)
 
-    for j in range(1, half):
-        w_relay(j).wait_recv()
-        w_relay(j).start()
-    for copy in own:
-        copy.wait()
     masks.wait()
 
     def make_bias(b, carry):
@@ -180,36 +269,37 @@
         return carry
 
     lax.fori_loop(0, blocks, make_bias, 0)
-    for j in range(half):
-        s = lax.rem(sib + 2 * j, feats)
+    for n in range(len(pairs) + 1):
+        s = flip(sib, 2 * n, feats)
         remote(w_ref, w_rows(s), w_send.at[0], w_recv.at[s], {"feat": sib}).wait_recv()
 
-    def project(c, carry):
-        for j in range(1, feats):
-            x_arrival(j, c).wait_recv()
+    def project(c):
+        size = parts[c][1]
+        for n in others:
+            x_arrival(n, c).wait_recv()
+        xg[f, piece(c)] = xst[f, piece(c)]
         taken = jnp.concatenate(
-            [xg[s, piece(c)].reshape(part * rows, depth) for s in range(feats)], axis=1
+            [xg[s, piece(c)].reshape(size * rows, depth) for s in range(feats)], axis=1
         )
         made = jnp.dot(taken, wg[...], preferred_element_type=jnp.float32)
-        hid[piece(c)] = made.astype(hid.dtype).reshape(part, rows, width)
-        return carry
-
-    lax.fori_loop(0, CHUNKS, project, 0)
-
-    def send_frontier(n, carry):
-        j = graphs - 1 - n
+        hid[piece(c)] = made.astype(hid.dtype).reshape(size, rows, width)
+
+    project(0)
+    for c in range(cap):
+        z_first(c).start()
+    project(1)
+    for n in range(1, graphs - 1):
+        j = order(n)
         to = graph_at(j)
         for c in range(cap):
-            stage[j, c] = hid[send_ref[to, c]]
+            stage[j, c] = hid[spot[send_ref[to, c]]]
             z_copy(j, c).start()
-        return carry
-
-    lax.fori_loop(0, graphs - 1, send_frontier, 0)
     for c in range(cap):
-        front[g, c] = hid[send_ref[g, c]]
-
-    def score_targets(c, carry):
-        mine = hid[piece(c)].reshape(part * rows, width)
+        front[g, c] = hid[spot[send_ref[g, c]]]
+
+    def score_targets(c):
+        size = parts[c][1]
+        mine = hid[piece(c)].reshape(size * rows, width)
         for h in range(HEADS):
             cols = slice(h * hw, (h + 1) * hw)
             both = lax.dot_general(
@@ -219,9 +309,8 @@
             )
             for r in range(relations):
                 target[h, r, piece(c)] = both[:, r * rows : (r + 1) * rows].reshape(
-                    part, rows, rows
+                    size, rows, rows
                 )
-        return carry
 
     def transform(j):
         q = graph_at(j)
@@ -240,7 +329,8 @@
         lax.fori_loop(0, relations, relation, 0)
 
     transform(0)
-    lax.fori_loop(0, CHUNKS, score_targets, 0)
+    for c in range(2):
+        score_targets(c)
 
     def receive(j, carry):
         for c in range(cap):
@@ -251,6 +341,7 @@
     lax.fori_loop(1, graphs, receive, 0)
 
     def attend(b, carry):
+        at = spot[b]
         index = []
         for k in range(lists):
             rel = rels_ref[b, k]
@@ -263,7 +354,7 @@
             top = None
             for k in range(lists):
                 rel, place = index[k]
-                raw = (target[h, rel, b] + scores[place, h : h + 1, :]) + bias[b, k]
+                raw = (target[h, rel, at] + scores[place, h : h + 1, :]) + bias[b, k]
                 raws[h, k] = raw
                 top = raw if top is None else jnp.maximum(top, raw)
             top = jnp.max(top, axis=1, keepdims=True)
@@ -275,7 +366,7 @@
         for h in range(HEADS):
             cols = slice(h * hw, (h + 1) * hw)
             summed = jnp.dot(weights[h], stack[h], preferred_element_type=jnp.float32)
-            mixed = summed[:, :hw] / summed[:, hw:] + hid[b, :, cols].astype(jnp.float32)
+            mixed = summed[:, :hw] / summed[:, hw:] + hid[at, :, cols].astype(jnp.float32)
             out_ref[b, :, cols] = jnp.where(
                 mixed > 0, mixed, jnp.exp(jnp.minimum(mixed, 0.0)) - 1.0
             ).astype(out_ref.dtype)
@@ -283,19 +374,20 @@
 
     lax.fori_loop(0, blocks, attend, 0)
 
-    for c in range(CHUNKS):
-        for j in range(1, feats):
-            x_copy(j, c).wait_send()
-    for j in range(half):
-        w_direct(j).wait_send()
-    for j in range(1, half):
-        w_relay(j).wait_send()
+    for n in others:
+        l_copy(n).wait_send()
+        for c in range(2):
+            x_copy(n, c).wait_send()
+    for n in range(len(pairs) + 1):
+        w_direct(n).wait_send()
+    for n in chips:
+        w_relay(n).wait_send()
     for j in range(1, graphs):
         for c in range(cap):
             z_copy(j, c).wait_send()
 
 
-def layer(send, rels, slots, x, w, relw, atts, attt, mask):
+def layer(send, tiles, rels, slots, x, w, relw, atts, attt, mask):
     feats, blocks, rows, depth = x.shape
     width = w.shape[1]
     graphs, cap = send.shape
@@ -310,10 +402,15 @@
     bf16, f32 = jnp.bfloat16, jnp.float32
     return pl.pallas_call(
         layer_kernel,
-        in_specs=[smem, smem, smem, anywhere, anywhere, whole, whole, whole, anywhere],
+        in_specs=[smem, whole, smem, smem, anywhere, anywhere, whole, whole, whole, anywhere],
         out_specs=whole,
         out_shape=jax.ShapeDtypeStruct((blocks, rows, width), bf16),
         scratch_shapes=[
+            pltpu.VMEM((feats,) + tiles.shape[1:], jnp.int32),
+            pltpu.SMEM((feats,) + tiles.shape[1:], jnp.int32),
+            pltpu.SMEM((blocks,), jnp.int32),
+            pltpu.VMEM((feats, blocks, rows, depth), bf16),
+            pltpu.VMEM((feats, blocks, rows, depth), bf16),
             pltpu.VMEM((feats, blocks, rows, depth), bf16),
             pltpu.VMEM((feats * depth, width), bf16),
             pltpu.VMEM((blocks, rows, width), bf16),
@@ -329,11 +426,13 @@
             pltpu.VMEM((HEADS, rows, lists * rows), bf16),
             pltpu.VMEM(mask.shape, jnp.int32),
             pltpu.VMEM(mask.shape, f32),
-            dma((3,)),
+            dma((5,)),
             dma((feats,)),
             dma((feats,)),
-            dma((feats, CHUNKS)),
-            dma((feats, CHUNKS)),
+            dma((2 * feats,)),
+            dma((feats,)),
+            dma((feats, 2)),
+            dma((feats, 2)),
             dma((graphs, cap)),
             dma((graphs, cap)),
         ],
@@ -341,14 +440,16 @@
             collective_id=0, has_side_effects=True, vmem_limit_bytes=58 << 20
         ),
         name="layer",
-    )(send, rels, slots, x, w, relw, atts, attt, mask)
+    )(send, tiles, rels, slots, x, w, relw, atts, attt, mask)
 
 
 def shards(x, w, relw, atts, attt, mask, rels, send, slots):
     rows = mask.shape[-1]
     blocks = mask.shape[0]
     x = x.reshape(-1, blocks, rows, x.shape[1])
-    out = layer(send[0], rels, slots, x, w, relw, atts, attt, mask)
+    cap = send.shape[2]
+    tiles = jnp.pad(send[0][:, None, :], ((0, 0), (0, 7), (0, 128 - cap)))
+    out = layer(send[0], tiles, rels, slots, x, w, relw, atts, attt, mask)
     return out.reshape(blocks * rows, -1)
 
 

time: 102 us -> 93.9 us (0.921)
  Pallas kernels: 99.4 us -> 90.1 us
  local copies, waits for them, and re-layouts: 2.26 us -> 3.55 us
    pallas_call x1, Pallas kernels: 99.4 us -> 90.1 us  [layer(): pl.pallas_call(layer_kernel, in_specs=[smem, whole, smem, smem, anywhere,...]
    pad x0 -> x1, local copies, waits for them, and re-layouts: none -> 1.29 us  [shards(): tiles = jnp.pad(send[0][:, None, :], ((0, 0), (0, 7), (0, 128 - cap)))]
where the time goes in v4:
time: 93.9 us; the launch traced here: 93.6 us
  Pallas kernels  90.1 us (96%)
  local copies, waits for them, and re-layouts  3.55 us (4%)
    pallas_call x1, Pallas kernels, layer(): pl.pallas_call(layer_kernel, in_specs=[smem, whole, smem, smem, anywhere,...  90.1 us
    unnamed x1, local copies, waits for them, and re-layouts  2.26 us

profile of v4, /device:TPU:0, one launch (start us, length us, event | category | flops | bytes accessed | tf_op | source)
XLA Modules:
  0.0 93.6 jit_solution(5377005891119850532)
XLA Ops:
  0.0 1.3 %pad.4.tiles_ref = s32[4,8,128]{2,1,0:T(8,128)} pad(s32[4,1,4]{2,1,0:T(1,128)} %bitcast.8, s32[]{:T(128)} %constant.0.clone.1), padding=0_0x0_7x0_124 | pad | bytes 16452 | tf_op jit(solution)/shard_map/jit(_pad)/pad | solution.py:451
  1.3 90.1 %layer.1 = bf16[8,128,512]{2,1,0:T(8,128)(2,1)} custom-call(s32[4,4]{1,0:T(4,128)} %bitcast.9, s32[4,8,128]{2,1,0:T(8,128)} %pad.4.tiles_ref, s32[8,12]{1,0:T(8,128)} %rels_ref.1, s32[8,12]{1,0:T(8,128)} %slots_ref.1, bf16[8,8,128,128]{3,2,1,0:T(8,128)(2,1)} %bitcast.7, bf16[128,512]{1,0:T(8,128)(2,1)} %w_ref.1, bf16[2,512,512]{2,1,0:T(8,128)(2,1)} %relw_ref.1, ...), custom_call_target="tpu_custom_call" | custom-call | tf_op jit(solution)/shard_map/layer/pallas_call | solution.py:403
  91.4 2.3 %copy.12 = bf16[1024,512]{1,0:T(8,128)(2,1)} copy(bf16[1024,512]{1,0:T(8,128)(2,1)} %bitcast.6) | data formatting | bytes 2097152

commit v5 on v4

--- a/solution.py
+++ b/solution.py
@@ -20,7 +20,6 @@
 
 def layer_kernel(
     send_ref,
-    tiles_ref,
     rels_ref,
     slots_ref,
     x_ref,
@@ -30,6 +29,7 @@
     attt_ref,
     mask_ref,
     out_ref,
+    tile,
     lists_got,
     lists_smem,
     spot,
@@ -45,9 +45,12 @@
     satt,
     tatt,
     target,
-    stack,
-    raws,
-    weights,
+    stack0,
+    stack1,
+    raws0,
+    raws1,
+    weights0,
+    weights1,
     live,
     bias,
     local_sem,
@@ -67,6 +70,7 @@
     lists = mask_ref.shape[1]
     slots = graphs * cap
     hw = width // HEADS
+    stack, raws, weights = (stack0, stack1), (raws0, raws1), (weights0, weights1)
     parts = ((0, cap), (cap, blocks - cap))
     g = lax.axis_index("graph")
     f = lax.axis_index("feat")
@@ -153,13 +157,13 @@
     def l_copy(n):
         to = feat_at(n)
         return remote(
-            tiles_ref.at[first], lists_got.at[f], l_send.at[n], l_recv.at[f], {"feat": to}
+            tile, lists_got.at[f], l_send.at[n], l_recv.at[f], {"feat": to}
         )
 
     def l_arrival(n):
         s = feat_at(n)
         return remote(
-            tiles_ref.at[first], lists_got.at[s], l_send.at[n], l_recv.at[s], {"feat": s}
+            tile, lists_got.at[s], l_send.at[n], l_recv.at[s], {"feat": s}
         )
 
     def z_first(c):
@@ -183,8 +187,13 @@
     own = [
         pltpu.make_async_copy(w_ref, w_rows(f), local_sem.at[0]),
         pltpu.make_async_copy(x_ref, xin, local_sem.at[1]),
-        pltpu.make_async_copy(tiles_ref.at[first], lists_got.at[f], local_sem.at[2]),
     ]
+    lane = lax.broadcasted_iota(jnp.int32, tile.shape, 1)
+    listed = jnp.zeros(tile.shape, jnp.int32)
+    for c in range(cap):
+        listed = jnp.where(lane == c, send_ref[first, c], listed)
+    tile[...] = listed
+    lists_got[f] = listed
     masks = pltpu.make_async_copy(mask_ref, live, local_sem.at[3])
     for copy in own:
         copy.start()
@@ -260,7 +269,6 @@
             tatt[n, r * rows : (r + 1) * rows, :] = jnp.broadcast_to(
                 half_att.astype(jnp.float32), (rows, width)
             ).astype(jnp.bfloat16)
-    stack[:, :, hw:] = jnp.ones((HEADS, lists * rows, hw), jnp.bfloat16)
 
     masks.wait()
 
@@ -340,39 +348,53 @@
 
     lax.fori_loop(1, graphs, receive, 0)
 
-    def attend(b, carry):
+    def attend(pair, carry):
+        for u in range(2):
+            attend_one(2 * pair + u, stack[u], raws[u], weights[u])
+        return carry
+
+    def attend_one(b, stacked, raw_buf, weight_buf):
         at = spot[b]
         index = []
         for k in range(lists):
             rel = rels_ref[b, k]
             index.append((rel, rel * slots + slots_ref[b, k]))
         for k in range(lists):
-            v = values[index[k][1]]
-            for h in range(HEADS):
-                stack[h, k * rows : (k + 1) * rows, :hw] = v[:, h * hw : (h + 1) * hw]
-        for h in range(HEADS):
-            top = None
-            for k in range(lists):
-                rel, place = index[k]
-                raw = (target[h, rel, at] + scores[place, h : h + 1, :]) + bias[b, k]
-                raws[h, k] = raw
-                top = raw if top is None else jnp.maximum(top, raw)
-            top = jnp.max(top, axis=1, keepdims=True)
-            top = jnp.broadcast_to(jnp.maximum(top, 0.2 * top), (rows, rows))
-            for k in range(lists):
-                raw = raws[h, k]
-                prob = jnp.exp2(jnp.maximum(raw, 0.2 * raw) - top)
-                weights[h, :, k * rows : (k + 1) * rows] = prob.astype(jnp.bfloat16)
-        for h in range(HEADS):
-            cols = slice(h * hw, (h + 1) * hw)
-            summed = jnp.dot(weights[h], stack[h], preferred_element_type=jnp.float32)
-            mixed = summed[:, :hw] / summed[:, hw:] + hid[at, :, cols].astype(jnp.float32)
-            out_ref[b, :, cols] = jnp.where(
-                mixed > 0, mixed, jnp.exp(jnp.minimum(mixed, 0.0)) - 1.0
-            ).astype(out_ref.dtype)
-        return carry
-
-    lax.fori_loop(0, blocks, attend, 0)
+            stacked[k * rows : (k + 1) * rows, :] = values[index[k][1]]
+        for m in range(HEADS // 2):
+            totals = []
+            for h in (2 * m, 2 * m + 1):
+                top = None
+                for k in range(lists):
+                    rel, place = index[k]
+                    raw = (target[h, rel, at] + scores[place, h : h + 1, :]) + bias[b, k]
+                    raw_buf[h, k] = raw
+                    top = raw if top is None else jnp.maximum(top, raw)
+                top = jnp.max(top, axis=1, keepdims=True)
+                top = jnp.broadcast_to(jnp.maximum(top, 0.2 * top), (rows, rows))
+                total = None
+                for k in range(lists):
+                    raw = raw_buf[h, k]
+                    prob = jnp.exp2(jnp.maximum(raw, 0.2 * raw) - top)
+                    total = prob if total is None else total + prob
+                    weight_buf[h * rows : (h + 1) * rows, k * rows : (k + 1) * rows] = (
+                        prob.astype(jnp.bfloat16)
+                    )
+                totals.append(jnp.sum(total, axis=1, keepdims=True))
+            both = jnp.dot(
+                weight_buf[2 * m * rows : (2 * m + 2) * rows, :],
+                stacked[:, 2 * m * hw : (2 * m + 2) * hw],
+                preferred_element_type=jnp.float32,
+            )
+            for n in range(2):
+                cols = slice((2 * m + n) * hw, (2 * m + n + 1) * hw)
+                summed = both[n * rows : (n + 1) * rows, n * hw : (n + 1) * hw]
+                mixed = summed * (1.0 / totals[n]) + hid[at, :, cols].astype(jnp.float32)
+                out_ref[b, :, cols] = jnp.where(
+                    mixed > 0, mixed, jnp.exp(jnp.minimum(mixed, 0.0)) - 1.0
+                ).astype(out_ref.dtype)
+
+    lax.fori_loop(0, blocks // 2, attend, 0)
 
     for n in others:
         l_copy(n).wait_send()
@@ -387,7 +409,7 @@
             z_copy(j, c).wait_send()
 
 
-def layer(send, tiles, rels, slots, x, w, relw, atts, attt, mask):
+def layer(send, rels, slots, x, w, relw, atts, attt, mask):
     feats, blocks, rows, depth = x.shape
     width = w.shape[1]
     graphs, cap = send.shape
@@ -402,12 +424,13 @@
     bf16, f32 = jnp.bfloat16, jnp.float32
     return pl.pallas_call(
         layer_kernel,
-        in_specs=[smem, whole, smem, smem, anywhere, anywhere, whole, whole, whole, anywhere],
+        in_specs=[smem, smem, smem, anywhere, anywhere, whole, whole, whole, anywhere],
         out_specs=whole,
         out_shape=jax.ShapeDtypeStruct((blocks, rows, width), bf16),
         scratch_shapes=[
-            pltpu.VMEM((feats,) + tiles.shape[1:], jnp.int32),
-            pltpu.SMEM((feats,) + tiles.shape[1:], jnp.int32),
+            pltpu.VMEM((8, 128), jnp.int32),
+            pltpu.VMEM((feats, 8, 128), jnp.int32),
+            pltpu.SMEM((feats, 8, 128), jnp.int32),
             pltpu.SMEM((blocks,), jnp.int32),
             pltpu.VMEM((feats, blocks, rows, depth), bf16),
             pltpu.VMEM((feats, blocks, rows, depth), bf16),
@@ -421,9 +444,12 @@
             pltpu.VMEM((relations, 16, width), bf16),
             pltpu.VMEM((2, relations * rows, width), bf16),
             pltpu.VMEM((HEADS, relations, blocks, rows, rows), f32),
-            pltpu.VMEM((HEADS, lists * rows, 2 * hw), bf16),
+            pltpu.VMEM((lists * rows, width), bf16),
+            pltpu.VMEM((lists * rows, width), bf16),
             pltpu.VMEM((HEADS, lists, rows, rows), f32),
-            pltpu.VMEM((HEADS, rows, lists * rows), bf16),
+            pltpu.VMEM((HEADS, lists, rows, rows), f32),
+            pltpu.VMEM((HEADS * rows, lists * rows), bf16),
+            pltpu.VMEM((HEADS * rows, lists * rows), bf16),
             pltpu.VMEM(mask.shape, jnp.int32),
             pltpu.VMEM(mask.shape, f32),
             dma((5,)),
@@ -440,16 +466,14 @@
             collective_id=0, has_side_effects=True, vmem_limit_bytes=58 << 20
         ),
         name="layer",
-    )(send, tiles, rels, slots, x, w, relw, atts, attt, mask)
+    )(send, rels, slots, x, w, relw, atts, attt, mask)
 
 
 def shards(x, w, relw, atts, attt, mask, rels, send, slots):
     rows = mask.shape[-1]
     blocks = mask.shape[0]
     x = x.reshape(-1, blocks, rows, x.shape[1])
-    cap = send.shape[2]
-    tiles = jnp.pad(send[0][:, None, :], ((0, 0), (0, 7), (0, 128 - cap)))
-    out = layer(send[0], tiles, rels, slots, x, w, relw, atts, attt, mask)
+    out = layer(send[0], rels, slots, x, w, relw, atts, attt, mask)
     return out.reshape(blocks * rows, -1)
 
 

time: 93.9 us -> 93.1 us (level)
  local copies, waits for them, and re-layouts: 3.55 us -> 2.26 us
    pad x1 -> x0, local copies, waits for them, and re-layouts: 1.29 us -> none  [shards(): tiles = jnp.pad(send[0][:, None, :], ((0, 0), (0, 7), (0, 128 - cap)))]
where the time goes in v5:
time: 93.1 us; the launch traced here: 92.9 us
  Pallas kernels  90.6 us (97%)
  local copies, waits for them, and re-layouts  2.26 us (2%)
    pallas_call x1, Pallas kernels, layer(): pl.pallas_call(layer_kernel, in_specs=[smem, smem, smem, anywhere, anywhe...  90.6 us
    unnamed x1, local copies, waits for them, and re-layouts  2.26 us

profile of v5, /device:TPU:0, one launch (start us, length us, event | category | flops | bytes accessed | tf_op | source)
XLA Modules:
  0.0 92.9 jit_solution(8717515806500712270)
XLA Ops:
  0.0 90.6 %layer.1 = bf16[8,128,512]{2,1,0:T(8,128)(2,1)} custom-call(s32[4,4]{1,0:T(4,128)} %bitcast.5, s32[8,12]{1,0:T(8,128)} %rels_ref.1, s32[8,12]{1,0:T(8,128)} %slots_ref.1, bf16[8,8,128,128]{3,2,1,0:T(8,128)(2,1)} %bitcast.4, bf16[128,512]{1,0:T(8,128)(2,1)} %w_ref.1, bf16[2,512,512]{2,1,0:T(8,128)(2,1)} %relw_ref.1, f32[2,512]{1,0:T(2,128)} %atts_ref.1, ...), custom_call_target="tpu_custom_call" | custom-call | tf_op jit(solution)/shard_map/layer/pallas_call | solution.py:425
  90.6 2.3 %copy.11 = bf16[1024,512]{1,0:T(8,128)(2,1)} copy(bf16[1024,512]{1,0:T(8,128)(2,1)} %bitcast.3) | data formatting | bytes 2097152

commit v6 on v5

--- a/solution.py
+++ b/solution.py
@@ -1,5 +1,3 @@
-import math
-
 import jax
 import jax.numpy as jnp
 from jax import lax
@@ -8,7 +6,6 @@
 from jax.sharding import PartitionSpec as P
 
 HEADS = 4
-LOG2E = math.log2(math.e)
 NT = (((1,), (1,)), ((), ()))
 
 
@@ -262,10 +259,10 @@
     for r in range(relations):
         halves = [
             jnp.where(head_of == row_of, half_att.astype(jnp.float32), 0.0)
-            for half_att in split_bf16(atts_ref[r : r + 1, :] * LOG2E)
+            for half_att in split_bf16(atts_ref[r : r + 1, :])
         ]
         satt[r] = jnp.concatenate(halves, axis=0).astype(jnp.bfloat16)
-        for n, half_att in enumerate(split_bf16(attt_ref[r : r + 1, :] * LOG2E)):
+        for n, half_att in enumerate(split_bf16(attt_ref[r : r + 1, :])):
             tatt[n, r * rows : (r + 1) * rows, :] = jnp.broadcast_to(
                 half_att.astype(jnp.float32), (rows, width)
             ).astype(jnp.bfloat16)
@@ -292,9 +289,18 @@
         made = jnp.dot(taken, wg[...], preferred_element_type=jnp.float32)
         hid[piece(c)] = made.astype(hid.dtype).reshape(size, rows, width)
 
-    project(0)
-    for c in range(cap):
+    for n in others:
+        x_arrival(n, 0).wait_recv()
+    xg[f, piece(0)] = xst[f, piece(0)]
+
+    def project_one(c, carry):
+        taken = jnp.concatenate([xg[s, c] for s in range(feats)], axis=1)
+        made = jnp.dot(taken, wg[...], preferred_element_type=jnp.float32)
+        hid[c] = made.astype(hid.dtype)
         z_first(c).start()
+        return carry
+
+    lax.fori_loop(0, cap, project_one, 0)
     project(1)
     for n in range(1, graphs - 1):
         j = order(n)
@@ -363,19 +369,22 @@
             stacked[k * rows : (k + 1) * rows, :] = values[index[k][1]]
         for m in range(HEADS // 2):
             totals = []
-            for h in (2 * m, 2 * m + 1):
-                top = None
-                for k in range(lists):
-                    rel, place = index[k]
-                    raw = (target[h, rel, at] + scores[place, h : h + 1, :]) + bias[b, k]
+            pair = (2 * m, 2 * m + 1)
+            tops = [None, None]
+            for k in range(lists):
+                rel, place = index[k]
+                closed = bias[b, k]
+                for n, h in enumerate(pair):
+                    raw = (target[h, rel, at] + scores[place, h : h + 1, :]) + closed
                     raw_buf[h, k] = raw
-                    top = raw if top is None else jnp.maximum(top, raw)
-                top = jnp.max(top, axis=1, keepdims=True)
-                top = jnp.broadcast_to(jnp.maximum(top, 0.2 * top), (rows, rows))
+                    tops[n] = raw if k == 0 else jnp.maximum(tops[n], raw)
+            tops = [jnp.max(top, axis=1, keepdims=True) for top in tops]
+            tops = [jnp.broadcast_to(jnp.maximum(top, 0.2 * top), (rows, rows)) for top in tops]
+            for n, h in enumerate(pair):
                 total = None
                 for k in range(lists):
                     raw = raw_buf[h, k]
-                    prob = jnp.exp2(jnp.maximum(raw, 0.2 * raw) - top)
+                    prob = jnp.exp(jnp.maximum(raw, 0.2 * raw) - tops[n])
                     total = prob if total is None else total + prob
                     weight_buf[h * rows : (h + 1) * rows, k * rows : (k + 1) * rows] = (
                         prob.astype(jnp.bfloat16)

time: 93.1 us -> 93.3 us (level)
  no operation moved by 1% of the time
where the time goes in v6:
time: 93.3 us; the launch traced here: 93.1 us
  Pallas kernels  90.8 us (97%)
  local copies, waits for them, and re-layouts  2.26 us (2%)
    pallas_call x1, Pallas kernels, layer(): pl.pallas_call(layer_kernel, in_specs=[smem, smem, smem, anywhere, anywhe...  90.8 us
    unnamed x1, local copies, waits for them, and re-layouts  2.26 us

profile of v6, /device:TPU:0, one launch (start us, length us, event | category | flops | bytes accessed | tf_op | source)
XLA Modules:
  0.0 93.1 jit_solution(429281042974376554)
XLA Ops:
  0.0 90.8 %layer.1 = bf16[8,128,512]{2,1,0:T(8,128)(2,1)} custom-call(s32[4,4]{1,0:T(4,128)} %bitcast.5, s32[8,12]{1,0:T(8,128)} %rels_ref.1, s32[8,12]{1,0:T(8,128)} %slots_ref.1, bf16[8,8,128,128]{3,2,1,0:T(8,128)(2,1)} %bitcast.4, bf16[128,512]{1,0:T(8,128)(2,1)} %w_ref.1, bf16[2,512,512]{2,1,0:T(8,128)(2,1)} %relw_ref.1, f32[2,512]{1,0:T(2,128)} %atts_ref.1, ...), custom_call_target="tpu_custom_call" | custom-call | tf_op jit(solution)/shard_map/layer/pallas_call | solution.py:434
  90.8 2.3 %copy.11 = bf16[1024,512]{1,0:T(8,128)(2,1)} copy(bf16[1024,512]{1,0:T(8,128)(2,1)} %bitcast.3) | data formatting | bytes 2097152

commit v7 on v6

--- a/solution.py
+++ b/solution.py
@@ -103,7 +103,7 @@
         return flip(g, j, graphs)
 
     def order(n):
-        return graphs - 1 - n + jnp.where(inner, 1 if n else 2 - graphs, 0)
+        return jnp.where(inner, n + 1, graphs - 1 - n)
 
     def w_rows(s):
         return wg.at[pl.ds(pl.multiple_of(s * depth, depth), depth)]

time: 93.3 us -> 90.2 us (0.967)
  the two profiles are of different devices: /device:TPU:0 before, /device:TPU:17 now
where the time goes in v7:
time: 90.2 us; the launch traced here: 90 us
  Pallas kernels  87.7 us (97%)
  local copies, waits for them, and re-layouts  2.26 us (3%)
    pallas_call x1, Pallas kernels, layer(): pl.pallas_call(layer_kernel, in_specs=[smem, smem, smem, anywhere, anywhe...  87.7 us
    unnamed x1, local copies, waits for them, and re-layouts  2.26 us

profile of v7, /device:TPU:17, one launch (start us, length us, event | category | flops | bytes accessed | tf_op | source)
XLA Modules:
  0.0 90.0 jit_solution(18113015463341770762)
XLA Ops:
  0.0 87.7 %layer.1 = bf16[8,128,512]{2,1,0:T(8,128)(2,1)} custom-call(s32[4,4]{1,0:T(4,128)} %bitcast.5, s32[8,12]{1,0:T(8,128)} %rels_ref.1, s32[8,12]{1,0:T(8,128)} %slots_ref.1, bf16[8,8,128,128]{3,2,1,0:T(8,128)(2,1)} %bitcast.4, bf16[128,512]{1,0:T(8,128)(2,1)} %w_ref.1, bf16[2,512,512]{2,1,0:T(8,128)(2,1)} %relw_ref.1, f32[2,512]{1,0:T(2,128)} %atts_ref.1, ...), custom_call_target="tpu_custom_call" | custom-call | tf_op jit(solution)/shard_map/layer/pallas_call | solution.py:434
  87.7 2.3 %copy.11 = bf16[1024,512]{1,0:T(8,128)(2,1)} copy(bf16[1024,512]{1,0:T(8,128)(2,1)} %bitcast.3) | data formatting | bytes 2097152
